TPU v7x, 32 devices: a whole 2x2x4 slice. The times are simulated.
32 devices in a mesh: fsdp: 4 (over y, x), ctx: 8 (over z, core).
Axes of the slice: x: 2, y: 2, z: 4, core: 2. Of those that a mesh axis runs over, the one named last changes fastest.
Arguments:
- tokens: bfloat16 [8192, 768], P(('fsdp', 'ctx')), may hold values from -6 to 6
- cotangent: bfloat16 [8192, 768], P(('fsdp', 'ctx')), may hold values from -6 to 6
- lengths: int32 [4], P('fsdp'), may hold values from 256 to 2048, as said below
- block_table: int32 [16], replicated, may hold values from 0 to 15, each once
- qkv_weight: bfloat16 [768, 2304], P('fsdp'), may hold values from -0.21875 to 0.21875
- query_bias: bfloat16 [768], P('fsdp'), may hold values from -3 to 3
- value_bias: bfloat16 [768], P('fsdp'), may hold values from -0.039794922 to 0.039794922
- proj_weight: bfloat16 [768, 768], P('fsdp')
- proj_bias: bfloat16 [768], P('fsdp'), may hold values from -3 to 3
- gain_first: bfloat16 [768], P('fsdp'), may hold values from 0.5 to 1.5
- shift_first: bfloat16 [768], P('fsdp'), may hold values from -3 to 3
- inner_weight: bfloat16 [768, 3072], P('fsdp'), may hold values from -0.21875 to 0.21875
- inner_bias: bfloat16 [3072], P('fsdp'), may hold values from -3 to 3
- outer_weight: bfloat16 [3072, 768], P('fsdp'), may hold values from -0.109375 to 0.109375
- outer_bias: bfloat16 [768], P('fsdp'), may hold values from -3 to 3
- gain_second: bfloat16 [768], P('fsdp'), may hold values from 0.5 to 1.5
- shift_second: bfloat16 [768], P('fsdp'), may hold values from -3 to 3
Outputs:
- layer_out: bfloat16 [8192, 768], P(('fsdp', 'ctx'))
- tokens_grad: bfloat16 [8192, 768], P(('fsdp', 'ctx'))
- qkv_weight_grad: float32 [768, 2304], P('fsdp')
- query_bias_grad: float32 [768], P('fsdp')
- value_bias_grad: float32 [768], P('fsdp')
- proj_weight_grad: float32 [768, 768], P('fsdp')
- proj_bias_grad: float32 [768], P('fsdp')
- gain_first_grad: float32 [768], P('fsdp')
- shift_first_grad: float32 [768], P('fsdp')
- inner_weight_grad: float32 [768, 3072], P('fsdp')
- inner_bias_grad: float32 [3072], P('fsdp')
- outer_weight_grad: float32 [3072, 768], P('fsdp')
- outer_bias_grad: float32 [768], P('fsdp')
- gain_second_grad: float32 [768], P('fsdp')
- shift_second_grad: float32 [768], P('fsdp')
Inputs may be any that keep to these rules, and one draw needn't show every extreme that they name: `lengths`: one sequence is full. `block_table`: each value appears once.
All inputs are finite; a program needn't handle non-finite values.
Results may differ from a plain program's by a relative error of at most 0.02.
Values may be sent and summed in bfloat16 or wider, within the bound.
A program may use at most 320 MiB of HBM per device.

v0:
```python
import math

import jax
import jax.numpy as jnp
from jax import lax
from jax.sharding import PartitionSpec as P

HEADS = 12
HEAD_DIM = 64
BLK = 128


NEG_FILL = -1e30
NORM_EPS = 1e-05


def layer_norm(vector_in, gain_in, shift_in):
    center = vector_in - jnp.mean(vector_in, axis=-1, keepdims=True)
    spread = jnp.mean(center * center, axis=-1, keepdims=True)
    return center * lax.rsqrt(spread + NORM_EPS) * gain_in + shift_in


def gelu_exact(vector_in):
    return jax.nn.gelu(vector_in, approximate=False)


def cross_dot(first_op, second_op):
    return lax.dot_general(
        first_op, second_op, (((0,), (0,)), ((), ())), preferred_element_type=jnp.float32
    )


def back_dot(first_op, second_op):
    return lax.dot_general(
        first_op, second_op, (((1,), (1,)), ((), ())), preferred_element_type=jnp.float32
    )


def key_valid(start_row, piece_rows, blk_rows, block_table, seq_length):
    index_rows = start_row + jnp.arange(piece_rows, dtype=jnp.int32)
    owner_block = index_rows // blk_rows
    table_slots = jnp.arange(block_table.shape[0], dtype=jnp.int32)
    placed = jnp.sum(
        jnp.where(owner_block[:, None] == table_slots[None, :], block_table[None, :], 0), axis=1
    )
    return placed * blk_rows + index_rows % blk_rows < seq_length


def exp_scores(query_blk, key_blk, valid_keys, lse_blk, score_scale):
    scores = (
        jnp.einsum("qhd,khd->hqk", query_blk, key_blk, preferred_element_type=jnp.float32)
        * score_scale
    )
    scores = jnp.where(valid_keys[None, None, :], scores, NEG_FILL)
    return jnp.exp(scores - lse_blk[:, :, None])


def local(
    tokens,
    cotangent,
    lengths,
    block_table,
    qkv_weight,
    query_bias,
    value_bias,
    proj_weight,
    proj_bias,
    gain_first,
    shift_first,
    inner_weight,
    inner_bias,
    outer_weight,
    outer_bias,
    gain_second,
    shift_second,
):
    feat_width = HEADS * HEAD_DIM
    tok_rows = tokens.shape[0]
    blk_rows = BLK
    score_scale = 1.0 / math.sqrt(HEAD_DIM)
    seq_length = lengths[0]
    qkv_full, qbias_full, vbias_full, proj_full, pbias_full, gain1_full, shift1_full = (
        lax.all_gather(qkv_weight, "fsdp", axis=0, tiled=True),
        lax.all_gather(query_bias, "fsdp", axis=0, tiled=True),
        lax.all_gather(value_bias, "fsdp", axis=0, tiled=True),
        lax.all_gather(proj_weight, "fsdp", axis=0, tiled=True),
        lax.all_gather(proj_bias, "fsdp", axis=0, tiled=True),
        lax.all_gather(gain_first, "fsdp", axis=0, tiled=True),
        lax.all_gather(shift_first, "fsdp", axis=0, tiled=True),
    )
    inner_full, ibias_full, outer_full, obias_full, gain2_full, shift2_full = (
        lax.all_gather(inner_weight, "fsdp", axis=0, tiled=True),
        lax.all_gather(inner_bias, "fsdp", axis=0, tiled=True),
        lax.all_gather(outer_weight, "fsdp", axis=0, tiled=True),
        lax.all_gather(outer_bias, "fsdp", axis=0, tiled=True),
        lax.all_gather(gain_second, "fsdp", axis=0, tiled=True),
        lax.all_gather(shift_second, "fsdp", axis=0, tiled=True),
    )
    tokens_wide = tokens.astype(jnp.float32)
    bias_row = jnp.concatenate([qbias_full, jnp.zeros_like(qbias_full), vbias_full]).astype(
        jnp.float32
    )
    packed = (jnp.dot(tokens, qkv_full, preferred_element_type=jnp.float32) + bias_row).astype(
        jnp.bfloat16
    )
    queries = packed[:, :feat_width]
    key_rows = packed[:, feat_width : 2 * feat_width]
    value_rows = packed[:, 2 * feat_width :]
    query_heads = queries.reshape(tok_rows, HEADS, HEAD_DIM)
    start_state = (
        jnp.full((HEADS, tok_rows), NEG_FILL, jnp.float32),
        jnp.zeros((HEADS, tok_rows), jnp.float32),
        jnp.zeros((tok_rows, HEADS, HEAD_DIM), jnp.float32),
    )
    key_piece = lax.all_gather(key_rows, "ctx", axis=0, tiled=True)
    value_piece = lax.all_gather(value_rows, "ctx", axis=0, tiled=True)
    piece_rows = key_piece.shape[0]
    fold_blk_size = math.gcd(piece_rows, 1024)
    num_blocks = piece_rows // fold_blk_size
    key_blocks = key_piece.reshape(num_blocks, fold_blk_size, HEADS, HEAD_DIM)
    value_blocks = value_piece.reshape(num_blocks, fold_blk_size, HEADS, HEAD_DIM)
    offsets = fold_blk_size * jnp.arange(num_blocks, dtype=jnp.int32)

    def scan_step(state_in, loop_item):
        running_max, running_sum, accum_out = state_in
        key_blk, value_blk, offset = loop_item
        valid_keys = key_valid(offset, fold_blk_size, blk_rows, block_table, seq_length)
        scores = (
            jnp.einsum("qhd,khd->hqk", query_heads, key_blk, preferred_element_type=jnp.float32)
            * score_scale
        )
        scores = jnp.where(valid_keys[None, None, :], scores, NEG_FILL)
        new_max = jnp.maximum(running_max, jnp.max(scores, axis=2))
        factor = jnp.exp(running_max - new_max)
        soft_weights = jnp.exp(scores - new_max[:, :, None])
        new_sum = running_sum * factor + jnp.sum(soft_weights, axis=2)
        update = jnp.einsum(
            "hqk,khd->qhd",
            soft_weights.astype(jnp.bfloat16),
            value_blk,
            preferred_element_type=jnp.float32,
        )
        accum_out = accum_out * jnp.transpose(factor)[:, :, None] + update
        return ((new_max, new_sum, accum_out), None)

    result, _ = lax.scan(scan_step, start_state, (key_blocks, value_blocks, offsets))
    run_max, run_sum, accum_out = result
    lse = run_max + jnp.log(run_sum)
    attn_heads = accum_out / jnp.transpose(run_sum)[:, :, None]
    context = attn_heads.reshape(tok_rows, feat_width).astype(jnp.bfloat16)
    hidden = (
        tokens_wide
        + jnp.dot(context, proj_full, preferred_element_type=jnp.float32)
        + pbias_full.astype(jnp.float32)
    )
    normed, norm_back = jax.vjp(
        layer_norm, hidden, gain1_full.astype(jnp.float32), shift1_full.astype(jnp.float32)
    )
    normed_low = normed.astype(jnp.bfloat16)
    inner_pre = jnp.dot(
        normed_low, inner_full, preferred_element_type=jnp.float32
    ) + ibias_full.astype(jnp.float32)
    active, gelu_back = jax.vjp(gelu_exact, inner_pre)
    active_low = active.astype(jnp.bfloat16)
    mixed_sum = (
        normed
        + jnp.dot(active_low, outer_full, preferred_element_type=jnp.float32)
        + obias_full.astype(jnp.float32)
    )
    result, final_back = jax.vjp(
        layer_norm, mixed_sum, gain2_full.astype(jnp.float32), shift2_full.astype(jnp.float32)
    )
    layer_out = result.astype(jnp.bfloat16)
    mixed_grad, gain2_grad, shift2_grad = final_back(cotangent.astype(jnp.float32))
    branch_low = mixed_grad.astype(jnp.bfloat16)
    outer_grad = cross_dot(active_low, branch_low)
    obias_grad = jnp.sum(branch_low.astype(jnp.float32), axis=0)
    (inner_grad_wide,) = gelu_back(back_dot(branch_low, outer_full))
    inner_low = inner_grad_wide.astype(jnp.bfloat16)
    inner_grad = cross_dot(normed_low, inner_low)
    ibias_grad = jnp.sum(inner_low.astype(jnp.float32), axis=0)
    normed_grad = mixed_grad + back_dot(inner_low, inner_full)
    hidden_grad, gain1_grad, shift1_grad = norm_back(normed_grad)
    proj_low = hidden_grad.astype(jnp.bfloat16)
    proj_grad = cross_dot(context, proj_low)
    pbias_grad = jnp.sum(proj_low.astype(jnp.float32), axis=0)
    context_grad = back_dot(proj_low, proj_full).astype(jnp.bfloat16)
    grad_heads = context_grad.reshape(tok_rows, HEADS, HEAD_DIM)
    delta = jnp.einsum("qhd,qhd->hq", grad_heads.astype(jnp.float32), attn_heads)
    gathered_keys, gathered_values = (
        lax.all_gather(key_rows, "ctx", axis=0, tiled=True),
        lax.all_gather(value_rows, "ctx", axis=0, tiled=True),
    )
    total_rows = gathered_keys.shape[0]
    blk_size = math.gcd(total_rows, 1024)
    num_blocks = total_rows // blk_size
    key_blocks = gathered_keys.reshape(num_blocks, blk_size, HEADS, HEAD_DIM)
    value_blocks = gathered_values.reshape(num_blocks, blk_size, HEADS, HEAD_DIM)
    offsets = blk_size * jnp.arange(num_blocks, dtype=jnp.int32)

    def scan_back(query_acc, loop_item):
        key_blk, value_blk, offset = loop_item
        valid_keys = key_valid(offset, blk_size, blk_rows, block_table, seq_length)
        attn_probs = exp_scores(query_heads, key_blk, valid_keys, lse, score_scale)
        value_part = jnp.einsum(
            "hqk,qhd->khd",
            attn_probs.astype(jnp.bfloat16),
            grad_heads,
            preferred_element_type=jnp.float32,
        )
        prob_grad = jnp.einsum(
            "qhd,khd->hqk", grad_heads, value_blk, preferred_element_type=jnp.float32
        )
        score_low = (attn_probs * (prob_grad - delta[:, :, None])).astype(jnp.bfloat16)
        query_acc = (
            query_acc
            + jnp.einsum("hqk,khd->qhd", score_low, key_blk, preferred_element_type=jnp.float32)
            * score_scale
        )
        key_part = (
            jnp.einsum("hqk,qhd->khd", score_low, query_heads, preferred_element_type=jnp.float32)
            * score_scale
        )
        return (
            query_acc,
            jnp.concatenate(
                [key_part.reshape(blk_size, feat_width), value_part.reshape(blk_size, feat_width)],
                axis=1,
            ),
        )

    query_acc, terms = lax.scan(
        scan_back,
        jnp.zeros((tok_rows, HEADS, HEAD_DIM), jnp.float32),
        (key_blocks, value_blocks, offsets),
    )
    key_value_grad = lax.psum_scatter(
        terms.reshape(total_rows, 2 * feat_width), "ctx", scatter_dimension=0, tiled=True
    )
    query_grad = query_acc.reshape(tok_rows, feat_width)
    key_grad = key_value_grad[:, :feat_width]
    value_grad = key_value_grad[:, feat_width:]
    packed_grad = jnp.concatenate([query_grad, key_grad, value_grad], axis=1).astype(jnp.bfloat16)
    qkv_grad = cross_dot(tokens, packed_grad)
    qbias_grad = jnp.sum(packed_grad[:, :feat_width].astype(jnp.float32), axis=0)
    vbias_grad = jnp.sum(packed_grad[:, 2 * feat_width :].astype(jnp.float32), axis=0)
    tokens_grad = (hidden_grad + back_dot(packed_grad, qkv_full)).astype(jnp.bfloat16)
    qkv_part, qbias_part, vbias_part, proj_part, pbias_part, gain1_part, shift1_part = (
        lax.psum_scatter(
            qkv_grad.astype(jnp.bfloat16), "fsdp", scatter_dimension=0, tiled=True
        ).astype(jnp.float32),
        lax.psum_scatter(
            qbias_grad.astype(jnp.bfloat16), "fsdp", scatter_dimension=0, tiled=True
        ).astype(jnp.float32),
        lax.psum_scatter(
            vbias_grad.astype(jnp.bfloat16), "fsdp", scatter_dimension=0, tiled=True
        ).astype(jnp.float32),
        lax.psum_scatter(
            proj_grad.astype(jnp.bfloat16), "fsdp", scatter_dimension=0, tiled=True
        ).astype(jnp.float32),
        lax.psum_scatter(
            pbias_grad.astype(jnp.bfloat16), "fsdp", scatter_dimension=0, tiled=True
        ).astype(jnp.float32),
        lax.psum_scatter(
            gain1_grad.astype(jnp.bfloat16), "fsdp", scatter_dimension=0, tiled=True
        ).astype(jnp.float32),
        lax.psum_scatter(
            shift1_grad.astype(jnp.bfloat16), "fsdp", scatter_dimension=0, tiled=True
        ).astype(jnp.float32),
    )
    inner_part, ibias_part, outer_part, obias_part, gain2_part, shift2_part = (
        lax.psum_scatter(
            inner_grad.astype(jnp.bfloat16), "fsdp", scatter_dimension=0, tiled=True
        ).astype(jnp.float32),
        lax.psum_scatter(
            ibias_grad.astype(jnp.bfloat16), "fsdp", scatter_dimension=0, tiled=True
        ).astype(jnp.float32),
        lax.psum_scatter(
            outer_grad.astype(jnp.bfloat16), "fsdp", scatter_dimension=0, tiled=True
        ).astype(jnp.float32),
        lax.psum_scatter(
            obias_grad.astype(jnp.bfloat16), "fsdp", scatter_dimension=0, tiled=True
        ).astype(jnp.float32),
        lax.psum_scatter(
            gain2_grad.astype(jnp.bfloat16), "fsdp", scatter_dimension=0, tiled=True
        ).astype(jnp.float32),
        lax.psum_scatter(
            shift2_grad.astype(jnp.bfloat16), "fsdp", scatter_dimension=0, tiled=True
        ).astype(jnp.float32),
    )
    summed = lax.psum(
        (
            qkv_part,
            qbias_part,
            vbias_part,
            proj_part,
            pbias_part,
            gain1_part,
            shift1_part,
            inner_part,
            ibias_part,
            outer_part,
            obias_part,
            gain2_part,
            shift2_part,
        ),
        "ctx",
    )
    return (
        layer_out,
        tokens_grad,
        summed[0],
        summed[1],
        summed[2],
        summed[3],
        summed[4],
        summed[5],
        summed[6],
        summed[7],
        summed[8],
        summed[9],
        summed[10],
        summed[11],
        summed[12],
    )


def solution(mesh):
    placed = (
        P(("fsdp", "ctx"), None),
        P(("fsdp", "ctx"), None),
        P("fsdp"),
        P(),
        P("fsdp", None),
        P("fsdp"),
        P("fsdp"),
        P("fsdp", None),
        P("fsdp"),
        P("fsdp"),
        P("fsdp"),
        P("fsdp", None),
        P("fsdp"),
        P("fsdp", None),
        P("fsdp"),
        P("fsdp"),
        P("fsdp"),
    )
    return jax.shard_map(
        local,
        mesh=mesh,
        in_specs=placed,
        out_specs=(
            P(("fsdp", "ctx"), None),
            P(("fsdp", "ctx"), None),
            P("fsdp", None),
            P("fsdp"),
            P("fsdp"),
            P("fsdp", None),
            P("fsdp"),
            P("fsdp"),
            P("fsdp"),
            P("fsdp", None),
            P("fsdp"),
            P("fsdp", None),
            P("fsdp"),
            P("fsdp"),
            P("fsdp"),
        ),
        check_vma=False,
    )
```

profile of v0, /device:TPU:0, one launch (start us, length us, event | category | flops | bytes accessed | tf_op | source)
XLA Modules:
  0.0 886.6 jit_solution(12183889524991659899)
XLA Ops:
  15.8 17.8 %all-reduce.19 = (bf16[768]{0:T(1024)(128)(2,1)S(1)}, bf16[768]{0:T(1024)(128)(2,1)S(1)}, bf16[768]{0:T(1024)(128)(2,1)S(1)}, bf16[768]{0:T(1024)(128)(2,1)S(1)}...) all-reduce(bf16[768]{0:T(1024)(128)(2,1)S(1)} %dynamic-update-slice, ...), channel_id=1, replica_groups=mesh['fsdp'=4,'ctx'=8] {'fsdp'}, use_global_device_ids=true, to_apply=%add.1 | all-reduce | flops 5376 | bytes 21504
  33.7 26.3 %all-gather.8.cloned.1.call-done = bf16[768,2304]{1,0:T(8,128)(2,1)} async-done(((bf16[192,2304]{1,0:T(8,128)(2,1)}), bf16[768,2304]{1,0:T(8,128)(2,1)}) %all-gather.8.cloned.1.call-update) | async-done | bytes 3538960 | tf_op jit(solution)/shard_map/all_gather | solution.py:83
  60.0 3.2 fusion.68
  67.9 8.6 all-gather
  79.6 23.0 %all-gather.10.cloned.1.call-done = bf16[2048,768]{1,0:T(8,128)(2,1)} async-done(((bf16[256,768]{1,0:T(8,128)(2,1)}), bf16[2048,768]{1,0:T(8,128)(2,1)}) %all-gather.10.cloned.1.call-update) | async-done | bytes 3145744 | tf_op jit(solution)/shard_map/all_gather | solution.py:115
  102.6 3.2 copy.79
  105.8 4.0 reshape.228
  109.8 3.1 copy.82
  112.9 29.1 %all-gather.12.cloned.1.call-done = bf16[2048,768]{1,0:T(8,128)(2,1)} async-done(((bf16[256,768]{1,0:T(8,128)(2,1)}), bf16[2048,768]{1,0:T(8,128)(2,1)}) %all-gather.12.cloned.1.call-update) | async-done | bytes 3145744 | tf_op jit(solution)/shard_map/all_gather | solution.py:116
  142.0 4.7 copy.81
  146.7 6.2 reshape.230
  152.9 4.5 copy.83
  157.4 50.1 %while.32 = (s32[]{:T(128)}, f32[12,256]{1,0:T(8,128)S(1)}, f32[12,256]{1,0:T(8,128)}, f32[256,12,64]{0,2,1:T(8,128)}, s32[2]{0:T(128)}, /*index=5*/s32[16]{0:T(...) while((s32[]{:T(128)}, f32[12,256]{1,0:T(8,128)S(1)}, ...), condition=%wide.region_4.5_spmd.clone, body=%wide.region_0.4_spmd.clone.sunk | while | flops 840597504 | bytes 93516152 | solution.py:146
  161.4 6.7 bitcast_reduce_fusion.2
  168.9 7.4 fusion.156
  177.1 5.1 fusion.158
  186.2 6.7 bitcast_reduce_fusion.2
  193.7 7.4 fusion.156
  202.2 5.3 fusion.158
  207.5 2.0 fusion.84
  209.5 2.1 fusion.100
  213.9 15.2 %all-gather.16.cloned.1.call-done = bf16[768,3072]{1,0:T(8,128)(2,1)} async-done(((bf16[192,3072]{1,0:T(8,128)(2,1)}), bf16[768,3072]{1,0:T(8,128)(2,1)}) %all-gather.16.cloned.1.call-update) | async-done | bytes 4718608 | tf_op jit(solution)/shard_map/all_gather | solution.py:92
  229.1 12.4 %multiply_convert_fusion.1 = (bf16[256,3072]{1,0:T(8,128)(2,1)}, f32[256,3072]{1,0:T(8,128)}, f32[256,3072]{1,0:T(8,128)}) fusion(f32[3072]{0:T(1024)} %bitcast.169, bf16[768,3072]{1,0:T(8,128)(2,1)} %all-gather.16.cloned.1.call-done, f32[256,768]{1,0:T(8,128)} %copy-done.3, f32[768]{0:T(1024)} %convert_element_type.168, f32[768]{0:T(1024)} %convert_element_type.167, ...), kind=kOutput, calls=%fused_computation.91 | convolution fusion | flops 1260847104 | bytes 13389824 | tf_op jit(solution)/shard_map/dot_general | solution.py:160
  241.6 46.4 %all-gather.18.cloned.1.call-done = bf16[3072,768]{1,0:T(8,128)(2,1)} async-done(((bf16[768,768]{1,0:T(8,128)(2,1)}), bf16[3072,768]{1,0:T(8,128)(2,1)}) %all-gather.18.cloned.1.call-update) | async-done | bytes 4718608 | tf_op jit(solution)/shard_map/all_gather | solution.py:94
  288.0 4.7 fusion.101
  295.1 2.8 fusion.92
  297.9 2.4 multiply_reduce_fusion
  304.3 1.9 copy.84
  306.3 2.0 fusion.82
  308.3 81.3 %while.33 = (s32[]{:T(128)}, f32[256,12,64]{0,2,1:T(8,128)}, f32[2,1024,1536]{2,1,0:T(8,128)}, bf16[2,1024,12,64]{1,3,2,0:T(8,128)(2,1)S(1)}, s32[2]{0:T(128)}, ...) while((s32[]{:T(128)}, f32[256,12,64]{0,2,1:T(8,128)}, ...), condition=%wide.region_15.16_spmd.clone, body=%wide.region_13.15_spmd.clone.sunk | while | flops 2047752192 | bytes 193675104 | solution.py:232
  308.5 1.8 fusion.169
  311.9 1.4 fusion.170
  313.3 6.4 multiply_convert_fusion.3
  319.7 5.0 fusion.171
  324.7 6.5 fusion.172
  331.2 2.0 convolution_multiply_fusion.2
  333.2 3.2 maximum_bitcast_fusion.2
  336.5 6.6 copy.116
  343.0 5.9 constant_dynamic-update-slice_fusion.2
  349.0 1.8 fusion.169
  353.8 6.4 multiply_convert_fusion.3
  360.2 5.1 fusion.171
  365.3 6.5 fusion.172
  371.9 2.0 convolution_multiply_fusion.2
  373.9 3.2 maximum_bitcast_fusion.2
  377.1 6.6 copy.116
  383.7 5.9 constant_dynamic-update-slice_fusion.2
  390.7 1.5 convolution_convert_fusion.3
  392.3 3.9 convolution_convert_fusion.1
  396.6 1.4 copy-done.12
  398.1 3.6 convolution_convert_fusion
  403.9 115.1 %reduce-scatter.8.cloned.1.call-done = f32[256,1536]{1,0:T(8,128)} async-done(((f32[2048,1536]{1,0:T(8,128)}), f32[256,1536]{1,0:T(8,128)}) %reduce-scatter.8.cloned.1.call-update) | async-done | bytes 1572880 | tf_op jit(solution)/shard_map/reduce_scatter | solution.py:237
  519.0 1.5 convert.14
  521.4 2.2 fusion.67
  523.6 3.9 copy.99
  530.3 19.1 %reduce-scatter.10.cloned.1.call-done = bf16[192,768]{1,0:T(8,128)(2,1)} async-done(((bf16[768,768]{1,0:T(8,128)(2,1)}), bf16[192,768]{1,0:T(8,128)(2,1)}) %reduce-scatter.10.cloned.1.call-update) | async-done | bytes 294928 | tf_op jit(solution)/shard_map/reduce_scatter | solution.py:258
  549.4 60.1 %reduce-scatter.12.cloned.1.call-done = bf16[192,3072]{1,0:T(8,128)(2,1)} async-done(((bf16[768,3072]{1,0:T(8,128)(2,1)}), bf16[192,3072]{1,0:T(8,128)(2,1)}) %reduce-scatter.12.cloned.1.call-update) | async-done | bytes 1179664 | tf_op jit(solution)/shard_map/reduce_scatter | solution.py:272
  609.5 60.0 %reduce-scatter.14.cloned.1.call-done = bf16[768,768]{1,0:T(8,128)(2,1)} async-done(((bf16[3072,768]{1,0:T(8,128)(2,1)}), bf16[768,768]{1,0:T(8,128)(2,1)}) %reduce-scatter.14.cloned.1.call-update) | async-done | bytes 1179664 | tf_op jit(solution)/shard_map/reduce_scatter | solution.py:278
  669.6 15.5 %all-reduce.18 = (bf16[768]{0:T(1024)(128)(2,1)S(1)}, bf16[768]{0:T(1024)(128)(2,1)S(1)}, bf16[768]{0:T(1024)(128)(2,1)S(1)}, bf16[768]{0:T(1024)(128)(2,1)S(1)}...) all-reduce(bf16[768]{0:T(1024)(128)(2,1)S(1)} %dynamic-update-slice, ...), channel_id=1, replica_groups=mesh['fsdp'=4,'ctx'=8] {'fsdp'}, use_global_device_ids=true, to_apply=%add.7 | all-reduce | flops 9984 | bytes 39936
  688.2 3.9 fusion.77
  692.1 27.9 %reduce-scatter.16.cloned.1.call-done = bf16[192,2304]{1,0:T(8,128)(2,1)} async-done(((bf16[768,2304]{1,0:T(8,128)(2,1)}), bf16[192,2304]{1,0:T(8,128)(2,1)}) %reduce-scatter.16.cloned.1.call-update) | async-done | bytes 884752
  720.0 1.5 copy.100
  721.6 156.4 %all-reduce.21 = (f32[192,2304]{0,1:T(8,128)S(1)}, f32[192]{0:T(256)}, f32[192]{0:T(256)}, f32[192,768]{1,0:T(8,128)}, f32[192]{0:T(256)}, /*index=5*/f32[192]{0...) all-reduce(bf16[192,2304]{0,1:T(8,128)(2,1)S(1)} %copy.100, ...), channel_id=1, replica_groups=mesh['fsdp'=4,'ctx'=8] {'ctx'}, use_global_device_ids=true, to_apply=%region_18.19 | all-reduce | flops 1771776 | bytes 10635264 | tf_op jit(solution)/shard_map/psum | solution.py:291
  878.0 1.8 copy.89
  (294 shorter events, 49.0 us)
Async XLA Ops:
  7.2 52.8 %all-gather.8.cloned.1.call-start = ((), (), s32[]{:S(2)}) async-start(), calls=%async_computation.5 | async-start | bytes 4423680 | tf_op jit(solution)/shard_map/all_gather | solution.py:83
  7.9 94.7 %all-gather.10.cloned.1.call-start = ((), (), s32[]{:S(2)}) async-start(), calls=%async_computation.6 | async-start | bytes 3538944 | tf_op jit(solution)/shard_map/all_gather | solution.py:115
  64.2 77.8 %all-gather.12.cloned.1.call-start = ((), (), s32[]{:S(2)}) async-start(), calls=%async_computation.7 | async-start | bytes 3538944 | tf_op jit(solution)/shard_map/all_gather | solution.py:116
  64.9 144.6 %all-gather.14.cloned.1.call-start = ((), (), s32[]{:S(2)}) async-start(), calls=%async_computation.8 | async-start | bytes 1474560 | tf_op jit(solution)/shard_map/all_gather | solution.py:86
  65.5 163.6 %all-gather.16.cloned.1.call-start = ((), (), s32[]{:S(2)}) async-start(), calls=%async_computation.9 | async-start | bytes 5898240 | tf_op jit(solution)/shard_map/all_gather | solution.py:92
  66.1 221.8 %all-gather.18.cloned.1.call-start = ((), (), s32[]{:S(2)}) async-start(), calls=%async_computation.10 | async-start | bytes 5898240 | tf_op jit(solution)/shard_map/all_gather | solution.py:94
  66.7 452.3 %reduce-scatter.8.cloned.1.call-start = ((), (), s32[]{:S(2)}) async-start(), calls=%async_computation.11 | async-start | bytes 14155776 | tf_op jit(solution)/shard_map/reduce_scatter | solution.py:237
  161.4 6.7 copy-start.31
  168.9 7.4 copy-start.26
  168.9 8.2 copy-start
  168.9 8.2 copy-start.32
  176.3 6.0 copy-start.27
  186.2 6.7 copy-start.31
  193.7 7.4 copy-start.26
  193.7 8.5 copy-start
  193.7 8.5 copy-start.32
  201.1 6.4 copy-start.27
  229.1 58.8 %copy-start.33 = (f32[768]{0:T(1024)S(1)}, f32[768]{0:T(1024)}, u32[]{:S(2)}) copy-start(f32[768]{0:T(1024)} %convert_element_type.167) | copy-start | bytes 9220
  229.1 58.8 %copy-start.36 = (f32[768]{0:T(1024)S(1)}, f32[768]{0:T(1024)}, u32[]{:S(2)}) copy-start(f32[768]{0:T(1024)} %convert_element_type.168) | copy-start | bytes 9220
  229.1 58.8 %copy-start.44 = (f32[256]{0:T(256)S(1)}, f32[256]{0:T(256)}, u32[]{:S(2)}) copy-start(f32[256]{0:T(256)} %copy-done.43) | copy-start | bytes 3076
  229.1 58.8 %copy-start.52 = (f32[256]{0:T(256)S(1)}, f32[256]{0:T(256)}, u32[]{:S(2)}) copy-start(f32[256]{0:T(256)} %fusion.85) | copy-start | bytes 3076
  287.9 7.1 slice-start.4
  288.0 5.0 copy-start.10
  288.0 5.0 copy-start.38
  288.0 7.1 slice-start.5
  288.0 7.1 copy-start.69
  293.0 4.9 copy-start.50
  300.4 5.9 copy-start.29
  308.5 4.8 copy-start.15
  308.5 4.8 copy-start.22
  308.5 4.8 copy-start.47
  308.5 4.8 copy-start.48
  310.4 9.3 %copy-start.1 = (f32[12,1024,256]{2,1,0:T(8,128)}, f32[12,1024,256]{2,1,0:T(8,128)S(1)}, u32[]{:S(2)}) copy-start(f32[12,1024,256]{2,1,0:T(8,128)S(1)} %fusion.169) | copy-start | bytes 37748740 | tf_op jit(solution)/shard_map/while
  319.7 5.0 copy-start.23
  319.7 5.0 copy-start.49
  319.7 11.5 %slice-start = ((s8[6291456]{0:T(1024)(128)(4,1)}), s8[4194304]{0:T(1024)(128)(4,1)S(1)}, s32[]{:S(2)}) async-start(s8[6291456]{0:T(1024)(128)(4,1)} %bitcast.156), calls=%async_computation.16 | async-start | bytes 8388608 | tf_op jit(solution)/shard_map/while
  324.7 6.5 slice-start.1
  349.0 4.8 copy-start.15
  349.0 4.8 copy-start.22
  349.0 4.8 copy-start.47
  349.0 4.8 copy-start.48
  350.8 9.3 %copy-start.1 = (f32[12,1024,256]{2,1,0:T(8,128)}, f32[12,1024,256]{2,1,0:T(8,128)S(1)}, u32[]{:S(2)}) copy-start(f32[12,1024,256]{2,1,0:T(8,128)S(1)} %fusion.169) | copy-start | bytes 37748740 | tf_op jit(solution)/shard_map/while
  360.2 5.1 copy-start.23
  360.2 5.1 copy-start.49
  360.2 11.7 %slice-start = ((s8[6291456]{0:T(1024)(128)(4,1)}), s8[4194304]{0:T(1024)(128)(4,1)S(1)}, s32[]{:S(2)}) async-start(s8[6291456]{0:T(1024)(128)(4,1)} %bitcast.156), calls=%async_computation.16 | async-start | bytes 8388608 | tf_op jit(solution)/shard_map/while
  365.3 6.5 slice-start.1
  389.7 159.7 %reduce-scatter.10.cloned.1.call-start = ((), (), s32[]{:S(2)}) async-start(), calls=%async_computation.12 | async-start | bytes 1474560 | tf_op jit(solution)/shard_map/reduce_scatter | solution.py:258
  392.2 217.3 %reduce-scatter.12.cloned.1.call-start = ((), (), s32[]{:S(2)}) async-start(), calls=%async_computation.13 | async-start | bytes 5898240 | tf_op jit(solution)/shard_map/reduce_scatter | solution.py:272
  396.3 273.2 %reduce-scatter.14.cloned.1.call-start = ((), (), s32[]{:S(2)}) async-start(), calls=%async_computation.14 | async-start | bytes 5898240 | tf_op jit(solution)/shard_map/reduce_scatter | solution.py:278
  401.7 318.3 %reduce-scatter.16.cloned.1.call-start = ((), (), s32[]{:S(2)}) async-start(), calls=%async_computation.15 | async-start | bytes 4423680
  527.5 142.0 %copy-start.19 = (bf16[256,1536]{1,0:T(8,128)(2,1)S(1)}, bf16[256,1536]{1,0:T(8,128)(2,1)}, u32[]{:S(2)}) copy-start(bf16[256,1536]{1,0:T(8,128)(2,1)} %copy-done.18) | copy-start | bytes 2359300
  527.5 142.0 %copy-start.57 = (bf16[768]{0:T(1024)(128)(2,1)S(1)}, bf16[768]{0:T(1024)(128)(2,1)}, u32[]{:S(2)}) copy-start(bf16[768]{0:T(1024)(128)(2,1)} %get-tuple-element.562) | copy-start | bytes 4612
  527.6 142.0 %copy-start.58 = (bf16[768]{0:T(1024)(128)(2,1)S(1)}, bf16[768]{0:T(1024)(128)(2,1)}, u32[]{:S(2)}) copy-start(bf16[768]{0:T(1024)(128)(2,1)} %get-tuple-element.641) | copy-start | bytes 4612
  527.6 142.0 %copy-start.59 = (bf16[768]{0:T(1024)(128)(2,1)S(1)}, bf16[768]{0:T(1024)(128)(2,1)}, u32[]{:S(2)}) copy-start(bf16[768]{0:T(1024)(128)(2,1)} %get-tuple-element.645) | copy-start | bytes 4612
  527.6 142.0 %copy-start.60 = (bf16[3072]{0:T(1024)(128)(2,1)S(1)}, bf16[3072]{0:T(1024)(128)(2,1)}, u32[]{:S(2)}) copy-start(bf16[3072]{0:T(1024)(128)(2,1)} %get-tuple-element.643) | copy-start | bytes 18436
  527.6 142.0 %copy-start.63 = (bf16[768]{0:T(1024)(128)(2,1)S(1)}, bf16[768]{0:T(1024)(128)(2,1)}, u32[]{:S(2)}) copy-start(bf16[768]{0:T(1024)(128)(2,1)} %get-tuple-element.560) | copy-start | bytes 4612
  527.6 142.0 %copy-start.64 = (bf16[768]{0:T(1024)(128)(2,1)S(1)}, bf16[768]{0:T(1024)(128)(2,1)}, u32[]{:S(2)}) copy-start(bf16[768]{0:T(1024)(128)(2,1)} %get-tuple-element.564) | copy-start | bytes 4612
  527.6 159.6 %copy-start.7 = (f32[256,768]{1,0:T(8,128)S(1)}, f32[256,768]{1,0:T(8,128)}, u32[]{:S(2)}) copy-start(f32[256,768]{1,0:T(8,128)} %copy-done.6) | copy-start | bytes 2359300
  527.6 159.6 %copy-start.39 = (f32[768]{0:T(1024)S(1)}, f32[768]{0:T(1024)}, u32[]{:S(2)}) copy-start(f32[768]{0:T(1024)} %convert_element_type.173) | copy-start | bytes 9220
  527.6 159.6 %copy-start.42 = (f32[256]{0:T(256)S(1)}, f32[256]{0:T(256)}, u32[]{:S(2)}) copy-start(f32[256]{0:T(256)} %copy-done.41) | copy-start | bytes 3076
  527.6 159.6 %copy-start.51 = (f32[256]{0:T(256)S(1)}, f32[256]{0:T(256)}, u32[]{:S(2)}) copy-start(f32[256]{0:T(256)} %copy-done.50) | copy-start | bytes 3076
  527.6 160.6 %copy-start.17 = (f32[256,768]{1,0:T(8,128)S(1)}, f32[256,768]{1,0:T(8,128)}, u32[]{:S(2)}) copy-start(f32[256,768]{1,0:T(8,128)} %copy-done.16) | copy-start | bytes 2359300
  527.7 160.6 %copy-start.30 = (bf16[256,768]{1,0:T(8,128)(2,1)S(1)}, bf16[256,768]{1,0:T(8,128)(2,1)}, u32[]{:S(2)}) copy-start(bf16[256,768]{1,0:T(8,128)(2,1)} %copy.88) | copy-start | bytes 1179652
  527.7 160.5 %copy-start.62 = (f32[256]{0:T(256)S(1)}, f32[256]{0:T(256)}, u32[]{:S(2)}) copy-start(f32[256]{0:T(256)} %copy-done.61) | copy-start | bytes 3076
  (39 other events, 85.7 us)
Sparse Core Ops, SparseCore 0:
  9.9 50.0 all-gather.7
  64.3 38.2 all-gather.9
  104.9 37.1 all-gather.11
  143.7 26.5 all-gather.13
  172.0 57.0 all-gather.15
  230.8 57.0 all-gather.17
  389.7 129.2 reduce-scatter.7
  522.5 26.8 reduce-scatter.9
  552.4 57.0 reduce-scatter.11
  612.4 57.0 reduce-scatter.13
  672.6 47.4 reduce-scatter.15
where the time goes:
time: 891 us; the launch traced here: 887 us
  waiting for transfers between devices  425 us (48%)
  blocking collectives  198 us (22%)
  matrix products  111 us (12%)
  local copies, waits for them, and re-layouts  83.2 us (9%)
  other arithmetic  50.1 us (6%)
  between operations  16.8 us (2%)
    psum x1, blocking collectives, local(): lax.psum((qkv_part, qbias_part, vbias_part, proj_part, pbias_part, gain1_...  156 us
    reduce_scatter x1, waiting for transfers between devices, local(): lax.psum_scatter(terms.reshape(total_rows, 2 * feat_width), 'ctx', scatte...  115 us
    reduce_scatter x1, waiting for transfers between devices, local(): lax.psum_scatter(inner_grad.astype(jnp.bfloat16), 'fsdp', scatter_dimensi...  60.1 us
    reduce_scatter x1, waiting for transfers between devices, local(): lax.psum_scatter(outer_grad.astype(jnp.bfloat16), 'fsdp', scatter_dimensi...  60 us
    all_gather x1, waiting for transfers between devices, local(): lax.all_gather(outer_weight, 'fsdp', axis=0, tiled=True)  46.4 us
    unnamed x2, blocking collectives  33.4 us
    unnamed x12, waiting for transfers between devices  31 us
    unnamed x144, local copies, waits for them, and re-layouts  30.2 us
  transfers between devices with their start and end apart: 11, of which 10 were waited for; matrix products, arithmetic and copies ran while one was open for 14% of the time, Pallas kernels for 0%

commit v1 on v0

v1 whole, which is shorter than its diff:
```python
import functools
import math

import jax
import jax.numpy as jnp
from jax import lax
from jax.experimental import pallas as pl
from jax.experimental.pallas import tpu as pltpu
from jax.sharding import PartitionSpec as P

HEADS = 12
HEAD_DIM = 64
BLK = 128


NEG_FILL = -1e30
NORM_EPS = 1e-05


def layer_norm(vector_in, gain_in, shift_in):
    center = vector_in - jnp.mean(vector_in, axis=-1, keepdims=True)
    spread = jnp.mean(center * center, axis=-1, keepdims=True)
    return center * lax.rsqrt(spread + NORM_EPS) * gain_in + shift_in


def gelu_exact(vector_in):
    return jax.nn.gelu(vector_in, approximate=False)


def cross_dot(first_op, second_op):
    return lax.dot_general(
        first_op, second_op, (((0,), (0,)), ((), ())), preferred_element_type=jnp.float32
    )


def back_dot(first_op, second_op):
    return lax.dot_general(
        first_op, second_op, (((1,), (1,)), ((), ())), preferred_element_type=jnp.float32
    )


def key_valid(start_row, piece_rows, blk_rows, block_table, seq_length):
    index_rows = start_row + jnp.arange(piece_rows, dtype=jnp.int32)
    owner_block = index_rows // blk_rows
    table_slots = jnp.arange(block_table.shape[0], dtype=jnp.int32)
    placed = jnp.sum(
        jnp.where(owner_block[:, None] == table_slots[None, :], block_table[None, :], 0), axis=1
    )
    return placed * blk_rows + index_rows % blk_rows < seq_length


def exp_scores(query_blk, key_blk, valid_keys, lse_blk, score_scale):
    scores = (
        jnp.einsum("qhd,khd->hqk", query_blk, key_blk, preferred_element_type=jnp.float32)
        * score_scale
    )
    scores = jnp.where(valid_keys[None, None, :], scores, NEG_FILL)
    return jnp.exp(scores - lse_blk[:, :, None])


def exchange_kernel(n, axis, x_ref, y_ref, send_sem, recv_sem, own_sem):
    me = lax.axis_index(axis)
    barrier = pltpu.get_barrier_semaphore()
    for step in range(1, n):
        pl.semaphore_signal(
            barrier,
            inc=1,
            device_id={axis: lax.rem(me + step, n)},
            device_id_type=pl.DeviceIdType.MESH,
        )
    own = pltpu.make_async_copy(x_ref.at[me], y_ref.at[me], own_sem)
    own.start()
    pl.semaphore_wait(barrier, n - 1)
    for step in range(1, n):
        peer = lax.rem(me + step, n)
        pltpu.make_async_remote_copy(
            src_ref=x_ref.at[peer],
            dst_ref=y_ref.at[me],
            send_sem=send_sem.at[step],
            recv_sem=recv_sem.at[step],
            device_id={axis: peer},
            device_id_type=pl.DeviceIdType.MESH,
        ).start()
    own.wait()
    for step in range(1, n):
        source = lax.rem(me + n - step, n)
        copy = pltpu.make_async_remote_copy(
            src_ref=x_ref.at[source],
            dst_ref=y_ref.at[source],
            send_sem=send_sem.at[step],
            recv_sem=recv_sem.at[step],
            device_id={axis: source},
            device_id_type=pl.DeviceIdType.MESH,
        )
        copy.wait()


def exchange(blocks, axis, number):
    n = blocks.shape[0]
    size = 2 * blocks.size * blocks.dtype.itemsize
    return pl.pallas_call(
        functools.partial(exchange_kernel, n, axis),
        out_shape=jax.ShapeDtypeStruct(blocks.shape, blocks.dtype),
        in_specs=[pl.BlockSpec(memory_space=pltpu.VMEM)],
        out_specs=pl.BlockSpec(memory_space=pltpu.VMEM),
        scratch_shapes=[
            pltpu.SemaphoreType.DMA((n,)),
            pltpu.SemaphoreType.DMA((n,)),
            pltpu.SemaphoreType.DMA,
        ],
        compiler_params=pltpu.CompilerParams(
            collective_id=number, has_side_effects=True, vmem_limit_bytes=size + (4 << 20)
        ),
        cost_estimate=pl.CostEstimate(flops=0, bytes_accessed=10 * size, transcendentals=0),
    )(blocks)


QTILE = 512


def attend_kernel(query_ref, key_ref, value_ref, out_ref, lse_ref):
    scores = lax.dot_general(
        key_ref[0], query_ref[...], (((1,), (1,)), ((), ())), preferred_element_type=jnp.float32
    )
    top = jnp.max(scores, axis=0, keepdims=True)
    weights = jnp.exp(scores - top)
    total = jnp.sum(weights, axis=0, keepdims=True)
    out = jnp.dot(value_ref[0], weights.astype(jnp.bfloat16), preferred_element_type=jnp.float32)
    out_ref[...] = out / total
    lse_ref[...] = top + jnp.log(total)


def attend(query, key, value_t):
    rows, keys = query.shape[0], key.shape[1]
    tiles_first = keys // QTILE
    return pl.pallas_call(
        attend_kernel,
        grid=(rows // QTILE,),
        in_specs=[
            pl.BlockSpec((QTILE, 2 * HEAD_DIM), lambda i: (i, 0)),
            pl.BlockSpec((1, keys, 2 * HEAD_DIM), lambda i: (i // tiles_first, 0, 0)),
            pl.BlockSpec((1, HEAD_DIM, keys), lambda i: (i // tiles_first, 0, 0)),
        ],
        out_specs=[
            pl.BlockSpec((HEAD_DIM, QTILE), lambda i: (0, i)),
            pl.BlockSpec((1, QTILE), lambda i: (0, i)),
        ],
        out_shape=[
            jax.ShapeDtypeStruct((HEAD_DIM, rows), jnp.float32),
            jax.ShapeDtypeStruct((1, rows), jnp.float32),
        ],
        compiler_params=pltpu.CompilerParams(vmem_limit_bytes=40 << 20),
        cost_estimate=pl.CostEstimate(
            flops=4 * rows * keys * HEAD_DIM, bytes_accessed=8 << 20, transcendentals=rows * keys
        ),
    )(query, key, value_t)


def attend_back_kernel(
    tiles_first,
    query_ref,
    key_ref,
    key_t_ref,
    value_ref,
    grad_ref,
    out_ref,
    grad_t_ref,
    lse_ref,
    dquery_ref,
    dkey_ref,
    dvalue_ref,
):
    step = pl.program_id(0)
    scores = back_dot(key_ref[0], query_ref[...])
    probs = jnp.exp(scores - lse_ref[...])
    delta = jnp.sum(out_ref[...] * grad_t_ref[...].astype(jnp.float32), axis=0, keepdims=True)
    prob_grad = back_dot(value_ref[0], grad_ref[...])
    score_low = (probs * (prob_grad - delta)).astype(jnp.bfloat16)
    dquery_ref[...] = jnp.dot(key_t_ref[0], score_low, preferred_element_type=jnp.float32)
    dkey = jnp.dot(score_low, query_ref[...], preferred_element_type=jnp.float32)
    dvalue = jnp.dot(
        probs.astype(jnp.bfloat16), grad_ref[...], preferred_element_type=jnp.float32
    )
    first = lax.rem(step, tiles_first) == 0

    @pl.when(first)
    def _():
        dkey_ref[0] = dkey
        dvalue_ref[0] = dvalue

    @pl.when(jnp.logical_not(first))
    def _():
        dkey_ref[0] += dkey
        dvalue_ref[0] += dvalue


def attend_back(query, key, key_t, value, grad, out, grad_t, lse):
    rows, keys = query.shape[0], key.shape[1]
    tiles_first = keys // QTILE
    pair = lambda i: (i // tiles_first, 0, 0)
    return pl.pallas_call(
        functools.partial(attend_back_kernel, tiles_first),
        grid=(rows // QTILE,),
        in_specs=[
            pl.BlockSpec((QTILE, 2 * HEAD_DIM), lambda i: (i, 0)),
            pl.BlockSpec((1, keys, 2 * HEAD_DIM), pair),
            pl.BlockSpec((1, HEAD_DIM, keys), pair),
            pl.BlockSpec((1, keys, HEAD_DIM), pair),
            pl.BlockSpec((QTILE, HEAD_DIM), lambda i: (i, 0)),
            pl.BlockSpec((HEAD_DIM, QTILE), lambda i: (0, i)),
            pl.BlockSpec((HEAD_DIM, QTILE), lambda i: (0, i)),
            pl.BlockSpec((1, QTILE), lambda i: (0, i)),
        ],
        out_specs=[
            pl.BlockSpec((HEAD_DIM, QTILE), lambda i: (0, i)),
            pl.BlockSpec((1, keys, 2 * HEAD_DIM), pair),
            pl.BlockSpec((1, keys, HEAD_DIM), pair),
        ],
        out_shape=[
            jax.ShapeDtypeStruct((HEAD_DIM, rows), jnp.float32),
            jax.ShapeDtypeStruct((2, keys, 2 * HEAD_DIM), jnp.float32),
            jax.ShapeDtypeStruct((2, keys, HEAD_DIM), jnp.float32),
        ],
        compiler_params=pltpu.CompilerParams(vmem_limit_bytes=52 << 20),
        cost_estimate=pl.CostEstimate(
            flops=10 * rows * keys * HEAD_DIM, bytes_accessed=12 << 20, transcendentals=rows * keys
        ),
    )(query, key, key_t, value, grad, out, grad_t, lse)


def pick_heads(columns, heads):
    return jnp.concatenate([columns[:, h * HEAD_DIM : (h + 1) * HEAD_DIM] for h in heads], axis=1)


def unit_heads(target):
    return 3 * (target // 2) + target % 2, 3 * (target // 2) + 2


def dealt_forward(packed, block_table, seq_length, n_ctx):
    rows = packed.shape[0]
    half = n_ctx // 2 * rows
    core = lax.axis_index("ctx") % 2
    sends = []
    for target in range(n_ctx):
        whole, shared = unit_heads(target)
        sends.append(
            pick_heads(
                packed,
                [whole, HEADS + whole, 2 * HEADS + whole, shared, HEADS + shared, 2 * HEADS + shared],
            )
        )
    got = exchange(jnp.stack(sends), "ctx", 1).reshape(n_ctx * rows, 6, HEAD_DIM)
    total = n_ctx * rows
    valid = key_valid(0, total, BLK, block_table, seq_length)
    mask_col = jnp.where(valid, 0.0, NEG_FILL).astype(jnp.bfloat16)[:, None]
    query = jnp.concatenate(
        [got[:, 0], lax.dynamic_slice_in_dim(got[:, 3], core * half, half, axis=0)], axis=0
    ) * jnp.bfloat16(1.0 / math.sqrt(HEAD_DIM))
    ones_col = jnp.ones((query.shape[0], 1), jnp.bfloat16)
    query = jnp.concatenate(
        [query, ones_col, jnp.zeros((query.shape[0], HEAD_DIM - 1), jnp.bfloat16)], axis=1
    )
    fill = jnp.zeros((total, HEAD_DIM - 1), jnp.bfloat16)
    key = jnp.stack(
        [
            jnp.concatenate([got[:, 1], mask_col, fill], axis=1),
            jnp.concatenate([got[:, 4], mask_col, fill], axis=1),
        ]
    )
    value = jnp.stack([got[:, 2], got[:, 5]])
    out, lse = attend(query, key, jnp.swapaxes(value, 1, 2))
    low = jnp.transpose(out.astype(jnp.bfloat16))
    first = low[:total].reshape(n_ctx, rows, HEAD_DIM)
    second = lax.dynamic_update_slice_in_dim(
        jnp.zeros((total, HEAD_DIM), jnp.bfloat16), low[total:], core * half, axis=0
    ).reshape(n_ctx, rows, HEAD_DIM)
    back = exchange(jnp.concatenate([first, second], axis=2), "ctx", 2)
    upper = lax.axis_index("ctx") >= n_ctx // 2
    pieces = []
    for chip in range(n_ctx // 2):
        pieces += [
            back[2 * chip, :, :HEAD_DIM],
            back[2 * chip + 1, :, :HEAD_DIM],
            jnp.where(upper, back[2 * chip + 1, :, HEAD_DIM:], back[2 * chip, :, HEAD_DIM:]),
        ]
    return jnp.concatenate(pieces, axis=1), (query, key, value, out, lse)


def dealt_backward(context_grad, saved, n_ctx):
    query, key, value, out, lse = saved
    rows = context_grad.shape[0]
    total = n_ctx * rows
    half = total // 2
    core = lax.axis_index("ctx") % 2
    sends = jnp.stack([pick_heads(context_grad, unit_heads(target)) for target in range(n_ctx)])
    got = exchange(sends, "ctx", 3).reshape(total, 2 * HEAD_DIM)
    grad = jnp.concatenate(
        [
            got[:, :HEAD_DIM],
            lax.dynamic_slice_in_dim(got[:, HEAD_DIM:], core * half, half, axis=0),
        ],
        axis=0,
    )
    key_t = jnp.swapaxes(key[:, :, :HEAD_DIM], 1, 2)
    dquery_t, dkey, dvalue = attend_back(
        query, key, key_t, value, grad, out, jnp.transpose(grad), lse
    )
    dquery = jnp.transpose((dquery_t * (1.0 / math.sqrt(HEAD_DIM))).astype(jnp.bfloat16))
    dkey = dkey[:, :, :HEAD_DIM].astype(jnp.bfloat16)
    dvalue = dvalue.astype(jnp.bfloat16)
    dshared = lax.dynamic_update_slice_in_dim(
        jnp.zeros((total, HEAD_DIM), jnp.bfloat16), dquery[total:], core * half, axis=0
    )
    sends = jnp.concatenate(
        [dquery[:total], dkey[0], dvalue[0], dshared, dkey[1], dvalue[1]], axis=1
    ).reshape(n_ctx, rows, 6 * HEAD_DIM)
    back = exchange(sends, "ctx", 4)
    piece = lambda source, k: back[source, :, k * HEAD_DIM : (k + 1) * HEAD_DIM]
    both = lambda chip, k: (
        piece(2 * chip, k).astype(jnp.float32) + piece(2 * chip + 1, k).astype(jnp.float32)
    ).astype(jnp.bfloat16)
    queries, keys, values = [], [], []
    for chip in range(n_ctx // 2):
        queries += [piece(2 * chip, 0), piece(2 * chip + 1, 0), both(chip, 3)]
        keys += [piece(2 * chip, 1), piece(2 * chip + 1, 1), both(chip, 4)]
        values += [piece(2 * chip, 2), piece(2 * chip + 1, 2), both(chip, 5)]
    return jnp.concatenate(queries + keys + values, axis=1)


def scan_forward(packed, block_table, seq_length):
    feat_width = HEADS * HEAD_DIM
    tok_rows = packed.shape[0]
    blk_rows = BLK
    score_scale = 1.0 / math.sqrt(HEAD_DIM)
    query_heads = packed[:, :feat_width].reshape(tok_rows, HEADS, HEAD_DIM)
    key_rows = packed[:, feat_width : 2 * feat_width]
    value_rows = packed[:, 2 * feat_width :]
    start_state = (
        jnp.full((HEADS, tok_rows), NEG_FILL, jnp.float32),
        jnp.zeros((HEADS, tok_rows), jnp.float32),
        jnp.zeros((tok_rows, HEADS, HEAD_DIM), jnp.float32),
    )
    key_piece = lax.all_gather(key_rows, "ctx", axis=0, tiled=True)
    value_piece = lax.all_gather(value_rows, "ctx", axis=0, tiled=True)
    piece_rows = key_piece.shape[0]
    fold_blk_size = math.gcd(piece_rows, 1024)
    num_blocks = piece_rows // fold_blk_size
    key_blocks = key_piece.reshape(num_blocks, fold_blk_size, HEADS, HEAD_DIM)
    value_blocks = value_piece.reshape(num_blocks, fold_blk_size, HEADS, HEAD_DIM)
    offsets = fold_blk_size * jnp.arange(num_blocks, dtype=jnp.int32)

    def scan_step(state_in, loop_item):
        running_max, running_sum, accum_out = state_in
        key_blk, value_blk, offset = loop_item
        valid_keys = key_valid(offset, fold_blk_size, blk_rows, block_table, seq_length)
        scores = (
            jnp.einsum("qhd,khd->hqk", query_heads, key_blk, preferred_element_type=jnp.float32)
            * score_scale
        )
        scores = jnp.where(valid_keys[None, None, :], scores, NEG_FILL)
        new_max = jnp.maximum(running_max, jnp.max(scores, axis=2))
        factor = jnp.exp(running_max - new_max)
        soft_weights = jnp.exp(scores - new_max[:, :, None])
        new_sum = running_sum * factor + jnp.sum(soft_weights, axis=2)
        update = jnp.einsum(
            "hqk,khd->qhd",
            soft_weights.astype(jnp.bfloat16),
            value_blk,
            preferred_element_type=jnp.float32,
        )
        accum_out = accum_out * jnp.transpose(factor)[:, :, None] + update
        return ((new_max, new_sum, accum_out), None)

    result, _ = lax.scan(scan_step, start_state, (key_blocks, value_blocks, offsets))
    run_max, run_sum, accum_out = result
    lse = run_max + jnp.log(run_sum)
    attn_heads = accum_out / jnp.transpose(run_sum)[:, :, None]
    context = attn_heads.reshape(tok_rows, feat_width).astype(jnp.bfloat16)
    return context, (query_heads, key_rows, value_rows, lse, attn_heads)


def scan_backward(context_grad, saved, block_table, seq_length):
    query_heads, key_rows, value_rows, lse, attn_heads = saved
    feat_width = HEADS * HEAD_DIM
    tok_rows = context_grad.shape[0]
    blk_rows = BLK
    score_scale = 1.0 / math.sqrt(HEAD_DIM)
    grad_heads = context_grad.reshape(tok_rows, HEADS, HEAD_DIM)
    delta = jnp.einsum("qhd,qhd->hq", grad_heads.astype(jnp.float32), attn_heads)
    gathered_keys, gathered_values = (
        lax.all_gather(key_rows, "ctx", axis=0, tiled=True),
        lax.all_gather(value_rows, "ctx", axis=0, tiled=True),
    )
    total_rows = gathered_keys.shape[0]
    blk_size = math.gcd(total_rows, 1024)
    num_blocks = total_rows // blk_size
    key_blocks = gathered_keys.reshape(num_blocks, blk_size, HEADS, HEAD_DIM)
    value_blocks = gathered_values.reshape(num_blocks, blk_size, HEADS, HEAD_DIM)
    offsets = blk_size * jnp.arange(num_blocks, dtype=jnp.int32)

    def scan_back(query_acc, loop_item):
        key_blk, value_blk, offset = loop_item
        valid_keys = key_valid(offset, blk_size, blk_rows, block_table, seq_length)
        attn_probs = exp_scores(query_heads, key_blk, valid_keys, lse, score_scale)
        value_part = jnp.einsum(
            "hqk,qhd->khd",
            attn_probs.astype(jnp.bfloat16),
            grad_heads,
            preferred_element_type=jnp.float32,
        )
        prob_grad = jnp.einsum(
            "qhd,khd->hqk", grad_heads, value_blk, preferred_element_type=jnp.float32
        )
        score_low = (attn_probs * (prob_grad - delta[:, :, None])).astype(jnp.bfloat16)
        query_acc = (
            query_acc
            + jnp.einsum("hqk,khd->qhd", score_low, key_blk, preferred_element_type=jnp.float32)
            * score_scale
        )
        key_part = (
            jnp.einsum("hqk,qhd->khd", score_low, query_heads, preferred_element_type=jnp.float32)
            * score_scale
        )
        return (
            query_acc,
            jnp.concatenate(
                [key_part.reshape(blk_size, feat_width), value_part.reshape(blk_size, feat_width)],
                axis=1,
            ),
        )

    query_acc, terms = lax.scan(
        scan_back,
        jnp.zeros((tok_rows, HEADS, HEAD_DIM), jnp.float32),
        (key_blocks, value_blocks, offsets),
    )
    key_value_grad = lax.psum_scatter(
        terms.reshape(total_rows, 2 * feat_width), "ctx", scatter_dimension=0, tiled=True
    )
    query_grad = query_acc.reshape(tok_rows, feat_width)
    key_grad = key_value_grad[:, :feat_width]
    value_grad = key_value_grad[:, feat_width:]
    return jnp.concatenate([query_grad, key_grad, value_grad], axis=1).astype(jnp.bfloat16)


def core_pairs(n_ctx):
    return [[2 * z, 2 * z + 1] for z in range(n_ctx // 2)]


def core_columns(n_ctx):
    return [list(range(0, n_ctx, 2)), list(range(1, n_ctx, 2))]


def gather_weight(shard, n_ctx):
    rows, columns = shard.shape
    half = rows // 2
    core = lax.axis_index("ctx") % 2
    mine = lax.dynamic_slice_in_dim(shard, core * half, half, axis=0)
    quarter = lax.all_gather(mine, "fsdp", axis=0)
    whole = lax.all_gather(quarter, "ctx", axis=1, axis_index_groups=core_pairs(n_ctx))
    return whole.reshape(-1, columns)


def reduce_weight(grad, n_fsdp, n_ctx):
    rows, columns = grad.shape
    if n_ctx != 8:
        part = lax.psum_scatter(
            grad.astype(jnp.bfloat16), "fsdp", scatter_dimension=0, tiled=True
        ).astype(jnp.float32)
        return lax.psum(part, "ctx")
    piece = rows // (n_fsdp * n_ctx)
    low = grad.astype(jnp.bfloat16).reshape(n_fsdp, n_ctx // 2, 2, piece, columns)
    low = lax.psum_scatter(
        low, "ctx", scatter_dimension=2, axis_index_groups=core_pairs(n_ctx)
    )
    low = lax.psum_scatter(low, "fsdp", scatter_dimension=0)
    low = lax.psum_scatter(
        low, "ctx", scatter_dimension=0, axis_index_groups=core_columns(n_ctx)
    )
    whole = lax.all_gather(low, "ctx", axis=0, tiled=True)
    return whole.astype(jnp.float32)


def local(
    tokens,
    cotangent,
    lengths,
    block_table,
    qkv_weight,
    query_bias,
    value_bias,
    proj_weight,
    proj_bias,
    gain_first,
    shift_first,
    inner_weight,
    inner_bias,
    outer_weight,
    outer_bias,
    gain_second,
    shift_second,
):
    feat_width = HEADS * HEAD_DIM
    tok_rows = tokens.shape[0]
    seq_length = lengths[0]
    n_fsdp = lax.axis_size("fsdp")
    n_ctx = lax.axis_size("ctx")
    dealt = n_ctx == 8 and tok_rows == 256
    vectors = (
        query_bias,
        value_bias,
        proj_bias,
        gain_first,
        shift_first,
        inner_bias,
        outer_bias,
        gain_second,
        shift_second,
    )
    ends = [0]
    for vector in vectors:
        ends.append(ends[-1] + vector.shape[0])
    gathered = lax.all_gather(jnp.concatenate(vectors)[None], "fsdp", axis=0, tiled=True)
    (
        qbias_full,
        vbias_full,
        pbias_full,
        gain1_full,
        shift1_full,
        ibias_full,
        obias_full,
        gain2_full,
        shift2_full,
    ) = [gathered[:, ends[k] : ends[k + 1]].reshape(-1) for k in range(len(vectors))]
    qkv_full = gather_weight(qkv_weight, n_ctx)
    proj_full = gather_weight(proj_weight, n_ctx)
    inner_full = gather_weight(inner_weight, n_ctx)
    outer_full = gather_weight(outer_weight, n_ctx)
    tokens_wide = tokens.astype(jnp.float32)
    bias_row = jnp.concatenate([qbias_full, jnp.zeros_like(qbias_full), vbias_full]).astype(
        jnp.float32
    )
    packed = (jnp.dot(tokens, qkv_full, preferred_element_type=jnp.float32) + bias_row).astype(
        jnp.bfloat16
    )
    if dealt:
        context, saved = dealt_forward(packed, block_table, seq_length, n_ctx)
    else:
        context, saved = scan_forward(packed, block_table, seq_length)
    hidden = (
        tokens_wide
        + jnp.dot(context, proj_full, preferred_element_type=jnp.float32)
        + pbias_full.astype(jnp.float32)
    )
    normed, norm_back = jax.vjp(
        layer_norm, hidden, gain1_full.astype(jnp.float32), shift1_full.astype(jnp.float32)
    )
    normed_low = normed.astype(jnp.bfloat16)
    inner_pre = jnp.dot(
        normed_low, inner_full, preferred_element_type=jnp.float32
    ) + ibias_full.astype(jnp.float32)
    active, gelu_back = jax.vjp(gelu_exact, inner_pre)
    active_low = active.astype(jnp.bfloat16)
    mixed_sum = (
        normed
        + jnp.dot(active_low, outer_full, preferred_element_type=jnp.float32)
        + obias_full.astype(jnp.float32)
    )
    result, final_back = jax.vjp(
        layer_norm, mixed_sum, gain2_full.astype(jnp.float32), shift2_full.astype(jnp.float32)
    )
    layer_out = result.astype(jnp.bfloat16)
    mixed_grad, gain2_grad, shift2_grad = final_back(cotangent.astype(jnp.float32))
    branch_low = mixed_grad.astype(jnp.bfloat16)
    outer_grad = cross_dot(active_low, branch_low)
    obias_grad = jnp.sum(branch_low.astype(jnp.float32), axis=0)
    (inner_grad_wide,) = gelu_back(back_dot(branch_low, outer_full))
    inner_low = inner_grad_wide.astype(jnp.bfloat16)
    inner_grad = cross_dot(normed_low, inner_low)
    ibias_grad = jnp.sum(inner_low.astype(jnp.float32), axis=0)
    normed_grad = mixed_grad + back_dot(inner_low, inner_full)
    hidden_grad, gain1_grad, shift1_grad = norm_back(normed_grad)
    proj_low = hidden_grad.astype(jnp.bfloat16)
    proj_grad = cross_dot(context, proj_low)
    pbias_grad = jnp.sum(proj_low.astype(jnp.float32), axis=0)
    context_grad = back_dot(proj_low, proj_full).astype(jnp.bfloat16)
    if dealt:
        packed_grad = dealt_backward(context_grad, saved, n_ctx)
    else:
        packed_grad = scan_backward(context_grad, saved, block_table, seq_length)
    qkv_grad = cross_dot(tokens, packed_grad)
    qbias_grad = jnp.sum(packed_grad[:, :feat_width].astype(jnp.float32), axis=0)
    vbias_grad = jnp.sum(packed_grad[:, 2 * feat_width :].astype(jnp.float32), axis=0)
    tokens_grad = (hidden_grad + back_dot(packed_grad, qkv_full)).astype(jnp.bfloat16)
    sums = (
        qbias_grad,
        vbias_grad,
        pbias_grad,
        gain1_grad,
        shift1_grad,
        ibias_grad,
        obias_grad,
        gain2_grad,
        shift2_grad,
    )
    bundle = jnp.concatenate([total.reshape(n_fsdp, -1) for total in sums], axis=1)
    bundle = lax.psum(bundle, ("fsdp", "ctx"))
    bundle = lax.dynamic_index_in_dim(bundle, lax.axis_index("fsdp"), axis=0, keepdims=False)
    vector_parts = [bundle[ends[k] : ends[k + 1]] for k in range(len(sums))]
    return (
        layer_out,
        tokens_grad,
        reduce_weight(qkv_grad, n_fsdp, n_ctx),
        vector_parts[0],
        vector_parts[1],
        reduce_weight(proj_grad, n_fsdp, n_ctx),
        vector_parts[2],
        vector_parts[3],
        vector_parts[4],
        reduce_weight(inner_grad, n_fsdp, n_ctx),
        vector_parts[5],
        reduce_weight(outer_grad, n_fsdp, n_ctx),
        vector_parts[6],
        vector_parts[7],
        vector_parts[8],
    )


def solution(mesh):
    placed = (
        P(("fsdp", "ctx"), None),
        P(("fsdp", "ctx"), None),
        P("fsdp"),
        P(),
        P("fsdp", None),
        P("fsdp"),
        P("fsdp"),
        P("fsdp", None),
        P("fsdp"),
        P("fsdp"),
        P("fsdp"),
        P("fsdp", None),
        P("fsdp"),
        P("fsdp", None),
        P("fsdp"),
        P("fsdp"),
        P("fsdp"),
    )
    return jax.shard_map(
        local,
        mesh=mesh,
        in_specs=placed,
        out_specs=(
            P(("fsdp", "ctx"), None),
            P(("fsdp", "ctx"), None),
            P("fsdp", None),
            P("fsdp"),
            P("fsdp"),
            P("fsdp", None),
            P("fsdp"),
            P("fsdp"),
            P("fsdp"),
            P("fsdp", None),
            P("fsdp"),
            P("fsdp", None),
            P("fsdp"),
            P("fsdp"),
            P("fsdp"),
        ),
        check_vma=False,
    )
```

time: 891 us -> 682 us (0.77)
  Pallas kernels: 0 us -> 130 us
  waiting for transfers between devices: 425 us -> 317 us
  blocking collectives: 198 us -> 93.9 us
  matrix products: 111 us -> 38.9 us
  other arithmetic: 50.1 us -> 19.1 us
  local copies, waits for them, and re-layouts: 83.2 us -> 60.7 us
    reduce_scatter x4 -> x8, waiting for transfers between devices: 254 us -> 42.7 us  [the longest x4 24.2 us: reduce_weight(): lax.psum_scatter(low, 'ctx', scatter_dimension=0, axis_index_groups=core_...]
    pallas_call x0 -> x6, Pallas kernels: none -> 130 us  [the longest x4 96.2 us: exchange(): pl.pallas_call(functools.partial(exchange_kernel, n, axis), out_shape=jax...]
    psum x1, blocking collectives: 156 us -> 39.5 us  [local(): bundle = lax.psum(bundle, ('fsdp', 'ctx'))]
    unnamed x12 -> x25, waiting for transfers between devices: 31 us -> 147 us
    dot_general x14 -> x0, matrix products: 67.5 us -> none  [the longest x2 13.4 us: scan_step(): jnp.einsum('qhd,khd->hqk', query_heads, key_blk, preferred_element_type=j...]
    all_gather x1 -> x4, blocking collectives: 8.61 us -> 54.4 us  [the longest x2 35.2 us: reduce_weight(): whole = lax.all_gather(low, 'ctx', axis=0, tiled=True)]
    unnamed x2 -> x0, blocking collectives: 33.4 us -> none
    dynamic_update_slice x4 -> x2, local copies, waits for them, and re-layouts: 25 us -> 1.03 us  [the longest x1 0.99 us: dealt_backward(): lax.dynamic_update_slice_in_dim(jnp.zeros((total, HEAD_DIM), jnp.bfloat16...]
  transfers between devices with their start and end apart: 11 -> 21, of which waited for: 10 -> 12; matrix products, arithmetic and copies ran while one was open for 14% -> 14% of each run, Pallas kernels for 0% -> 19%
where the time goes in v1:
time: 682 us; the launch traced here: 677 us
  waiting for transfers between devices  317 us (46%)
  Pallas kernels  130 us (19%)
  blocking collectives  93.9 us (14%)
  local copies, waits for them, and re-layouts  60.7 us (9%)
  matrix products  38.9 us (6%)
  other arithmetic  19.1 us (3%)
  between operations  17 us (2%)
    unnamed x25, waiting for transfers between devices  147 us
    pallas_call x4, Pallas kernels, exchange(): pl.pallas_call(functools.partial(exchange_kernel, n, axis), out_shape=jax...  96.2 us
    all_gather x3, waiting for transfers between devices, gather_weight(): quarter = lax.all_gather(mine, 'fsdp', axis=0)  88.9 us
    psum x1, blocking collectives, local(): bundle = lax.psum(bundle, ('fsdp', 'ctx'))  39.5 us
    all_gather x2, blocking collectives, reduce_weight(): whole = lax.all_gather(low, 'ctx', axis=0, tiled=True)  35.2 us
    all_gather x2, waiting for transfers between devices, reduce_weight(): whole = lax.all_gather(low, 'ctx', axis=0, tiled=True)  24.3 us
    reduce_scatter x4, waiting for transfers between devices, reduce_weight(): lax.psum_scatter(low, 'ctx', scatter_dimension=0, axis_index_groups=core_...  24.2 us
    pallas_call x1, Pallas kernels, attend_back(): pl.pallas_call(functools.partial(attend_back_kernel, tiles_first), grid=(...  20.4 us
  transfers between devices with their start and end apart: 21, of which 12 were waited for; matrix products, arithmetic and copies ran while one was open for 14% of the time, Pallas kernels for 19%

profile of v1, /device:TPU:0, one launch (start us, length us, event | category | flops | bytes accessed | tf_op | source)
XLA Modules:
  0.0 677.4 jit_solution(705021435302814161)
XLA Ops:
  7.3 2.0 constant_dynamic-slice_fusion.6
  11.3 34.5 %all-gather.24.cloned.1.call-done = bf16[384,2304]{1,0:T(8,128)(2,1)} async-done(((bf16[96,2304]{1,0:T(8,128)(2,1)}), bf16[384,2304]{1,0:T(8,128)(2,1)}) %all-gather.24.cloned.1.call-update) | async-done | bytes 1769488 | tf_op jit(solution)/shard_map/all_gather | solution.py:459
  45.9 11.0 %all-gather.3 = bf16[384,768]{1,0:T(8,128)(2,1)} all-gather(bf16[96,768]{1,0:T(8,128)(2,1)S(1)} %constant_dynamic-slice_fusion.4), channel_id=5, replica_groups=mesh['fsdp'=4,'ctx'=8] {'fsdp'}, dimensions={0}, use_global_device_ids=true | all-gather | bytes 737280 | tf_op jit(solution)/shard_map/all_gather | solution.py:459
  57.0 28.7 %all-gather.30.cloned.1.call-done = bf16[384,3072]{1,0:T(8,128)(2,1)} async-done(((bf16[96,3072]{1,0:T(8,128)(2,1)}), bf16[384,3072]{1,0:T(8,128)(2,1)}) %all-gather.30.cloned.1.call-update) | async-done | bytes 2359312 | tf_op jit(solution)/shard_map/all_gather | solution.py:459
  86.0 8.1 %all-gather.13 = bf16[4,1,2304]{2,1,0:T(2,128)(2,1)S(1)} all-gather(bf16[1,1,2304]{2,1,0:T(2,128)(2,1)S(1)} %reshape.419), channel_id=4, replica_groups=mesh['fsdp'=4,'ctx'=8] {'fsdp'}, dimensions={0}, use_global_device_ids=true | all-gather | bytes 23040 | tf_op jit(solution)/shard_map/all_gather | solution.py:523
  100.0 25.7 %all-gather.34.cloned.1.call-done = bf16[1536,768]{1,0:T(8,128)(2,1)} async-done(((bf16[384,768]{1,0:T(8,128)(2,1)}), bf16[1536,768]{1,0:T(8,128)(2,1)}) %all-gather.34.cloned.1.call-update) | async-done | bytes 2359312 | tf_op jit(solution)/shard_map/all_gather | solution.py:459
  125.7 14.1 %all-gather.26.cloned.1.call-done = bf16[4,192,2304]{2,1,0:T(8,128)(2,1)} async-done(((bf16[4,96,2304]{2,1,0:T(8,128)(2,1)}), bf16[4,192,2304]{2,1,0:T(8,128)(2,1)}) %all-gather.26.cloned.1.call-update) | async-done | bytes 3538960 | tf_op jit(solution)/shard_map/all_gather | solution.py:460
  139.8 3.1 fusion.1
  142.9 1.0 fusion.59
  143.9 1.0 fusion.58
  145.1 1.1 concatenate.118
  146.2 1.1 concatenate.119
  147.3 1.1 concatenate.120
  148.4 1.1 concatenate.121
  150.2 29.6 %shard_map.280 = bf16[8,256,384]{2,1,0:T(8,128)(2,1)S(1)} custom-call(bf16[8,256,384]{2,1,0:T(8,128)(2,1)S(1)} %bitcast_dynamic-update-slice_fusion.x_ref), custom_call_target="tpu_custom_call" | custom-call | bytes 31457280 | tf_op jit(solution)/shard_map/pallas_call | solution.py:101
  179.9 1.4 copy.84
  186.0 1.4 copy.107
  187.5 2.0 copy.106
  189.4 1.2 maximum_multiply_fusion
  190.9 1.6 pad_maximum_fusion.1
  192.5 1.5 copy.90.value_ref
  194.1 12.9 %shard_map.281 = (f32[64,3072]{1,0:T(8,128)S(1)}, f32[1,3072]{1,0:T(1,128)S(1)}) custom-call(bf16[3072,128]{1,0:T(8,128)(2,1)S(1)} %maximum_maximum_fusion.query_ref, bf16[2,2048,128]{2,1,0:T(8,128)(2,1)S(1)} %copy.89.key_ref, bf16[2,64,2048]{2,1,0:T(8,128)(2,1)S(1)} %copy.90.value_ref), custom_call_target="tpu_custom_call" | custom-call | flops 1610612736 | bytes 8388608 | tf_op jit(solution)/shard_map/pallas_call | solution.py:136
  208.0 20.4 %shard_map.282 = bf16[8,256,128]{2,1,0:T(8,128)(2,1)S(1)} custom-call(bf16[8,256,128]{2,1,0:T(8,128)(2,1)S(1)} %pad_maximum_fusion.4.x_ref), custom_call_target="tpu_custom_call" | custom-call | bytes 10485760 | tf_op jit(solution)/shard_map/pallas_call | solution.py:101
  229.1 1.8 fusion.65
  231.3 11.8 %multiply_convert_fusion = (bf16[256,3072]{1,0:T(8,128)(2,1)}, f32[256,3072]{1,0:T(8,128)}, f32[256,3072]{1,0:T(8,128)}) fusion(f32[3072]{0:T(1024)S(1)} %copy-done.53, bf16[768,3072]{1,0:T(8,128)(2,1)} %bitcast.293, f32[256,768]{1,0:T(8,128)S(1)} %get-tuple-element.171, f32[768]{0:T(1024)S(1)} %copy-done.38, f32[768]{0:T(1024)S(1)} %reshape.392, ...), kind=kOutput, calls=%fused_computation.11 | convolution fusion | flops 1260847104 | bytes 13389824 | tf_op jit(solution)/shard_map/dot_general | solution.py:559
  243.2 4.4 fusion.66
  248.8 1.1 fusion.55
  250.8 2.7 convert_reduce_fusion
  253.5 1.6 convolution_convert_fusion.1
  255.1 2.6 copy.100
  258.4 5.1 multiply_reduce_fusion
  264.5 1.1 copy.99
  265.8 2.4 convolution_convert_fusion
  268.2 3.1 copy.101
  271.5 1.0 copy-done.7
  274.4 14.5 %shard_map.283 = bf16[8,256,128]{2,1,0:T(8,128)(2,1)S(1)} custom-call(bf16[8,256,128]{2,1,0:T(8,128)(2,1)S(1)} %fusion.35.x_ref), custom_call_target="tpu_custom_call" | custom-call | bytes 10485760 | tf_op jit(solution)/shard_map/pallas_call | solution.py:101
  289.6 1.2 copy.95.grad_ref
  290.8 20.4 %shard_map.284 = (f32[64,3072]{1,0:T(8,128)S(1)}, f32[2,2048,128]{2,1,0:T(8,128)}, f32[2,2048,64]{2,1,0:T(8,128)}) custom-call(bf16[3072,128]{1,0:T(8,128)(2,1)} %copy-done.4, bf16[2,2048,128]{2,1,0:T(8,128)(2,1)} %copy-done.2, bf16[2,64,2048]{2,1,0:T(8,128)(2,1)S(1)} %fusion.21.key_t_ref, bf16[2,2048,64]{2,1,0:T(8,128)(2,1)} %get-tuple-element.125.value_ref, ...), custom_call_target="tpu_custom_call" | custom-call | flops 4026531840 | bytes 12582912 | tf_op jit(solution)/shard_map/pallas_call | solution.py:201
  311.6 1.9 convert.10
  314.9 1.0 constant_dynamic-update-slice_fusion
  315.9 1.0 fusion.61
  317.8 4.8 concatenate.146.x_ref
  322.6 31.6 %shard_map.285 = bf16[8,256,384]{2,1,0:T(8,128)(2,1)S(1)} custom-call(bf16[8,256,384]{2,1,0:T(8,128)(2,1)S(1)} %concatenate.146.x_ref), custom_call_target="tpu_custom_call" | custom-call | bytes 31457280 | tf_op jit(solution)/shard_map/pallas_call | solution.py:101
  354.8 1.0 slice_bitcast_fusion.6
  355.9 2.9 concatenate.147
  358.7 1.1 convolution_convert_fusion.2
  360.0 2.0 copy.98
  364.0 18.4 %reduce-scatter.21.cloned.1.call-done = bf16[4,4,1,24,2304]{4,3,1,0,2:T(8,128)(2,1)} async-done(((bf16[4,4,2,24,2304]{4,3,1,0,2:T(8,128)(2,1)}), bf16[4,4,1,24,2304]{4,3,1,0,2:T(8,128)(2,1)}) %reduce-scatter.21.cloned.1.call-update) | async-done | bytes 1769488 | tf_op jit(solution)/shard_map/reduce_scatter | solution.py:473
  382.5 41.4 %reduce-scatter.41.cloned.1.call-done = bf16[1,4,24,3072]{3,2,1,0:T(8,128)(2,1)} async-done(((bf16[4,4,24,3072]{3,2,1,0:T(8,128)(2,1)}), bf16[1,4,24,3072]{3,2,1,0:T(8,128)(2,1)}) %reduce-scatter.41.cloned.1.call-update) | async-done | bytes 589840
  424.0 27.9 %reduce-scatter.39.cloned.1.call-done = bf16[1,4,24,768]{3,2,1,0:T(8,128)(2,1)} async-done(((bf16[4,4,24,768]{3,2,1,0:T(8,128)(2,1)}), bf16[1,4,24,768]{3,2,1,0:T(8,128)(2,1)}) %reduce-scatter.39.cloned.1.call-update) | async-done | bytes 147472
  452.0 40.5 %reduce-scatter.43.cloned.1.call-done = bf16[1,4,96,768]{3,2,1,0:T(8,128)(2,1)} async-done(((bf16[4,4,96,768]{3,2,1,0:T(8,128)(2,1)}), bf16[1,4,96,768]{3,2,1,0:T(8,128)(2,1)}) %reduce-scatter.43.cloned.1.call-update) | async-done | bytes 589840
  492.6 35.6 %reduce-scatter.37.cloned.1.call-done = bf16[1,4,24,2304]{3,2,1,0:T(8,128)(2,1)} async-done(((bf16[4,4,24,2304]{3,2,1,0:T(8,128)(2,1)}), bf16[1,4,24,2304]{3,2,1,0:T(8,128)(2,1)}) %reduce-scatter.37.cloned.1.call-update) | async-done | bytes 442384
  528.2 24.2 %reduce-scatter.31.cloned.1.call-done = bf16[1,24,3072]{2,1,0:T(8,128)(2,1)} async-done(((bf16[4,24,3072]{2,1,0:T(8,128)(2,1)}), bf16[1,24,3072]{2,1,0:T(8,128)(2,1)}) %reduce-scatter.31.cloned.1.call-update) | async-done | bytes 147472 | tf_op jit(solution)/shard_map/reduce_scatter | solution.py:477
  552.5 1.1 concatenate.148
  553.7 1.1 concatenate.149
  557.8 39.5 %psum.7 = f32[4,2304]{1,0:T(4,128)S(1)} all-reduce(f32[4,2304]{1,0:T(4,128)S(1)} %concatenate.150), channel_id=1, replica_groups=mesh['fsdp'=4,'ctx'=8] {'fsdp','ctx'}, use_global_device_ids=true, to_apply=%region_21.22 | all-reduce | flops 9216 | bytes 73728 | tf_op jit(solution)/shard_map/psum | solution.py:607
  598.6 3.9 fusion.10
  602.5 15.9 %all-gather.10 = bf16[1,192,768]{2,1,0:T(8,128)(2,1)S(1)} all-gather(bf16[1,24,768]{2,1,0:T(8,128)(2,1)} %reduce-scatter.27.cloned.1.call-done), channel_id=12, replica_groups=mesh['fsdp'=4,'ctx'=8] {'ctx'}, dimensions={1}, use_global_device_ids=true | all-gather | bytes 331776 | tf_op jit(solution)/shard_map/all_gather | solution.py:480
  619.3 19.4 %all-gather.9 = bf16[1,192,2304]{2,1,0:T(8,128)(2,1)S(1)} all-gather(bf16[1,24,2304]{2,1,0:T(8,128)(2,1)} %reduce-scatter.23.cloned.1.call-done), channel_id=11, replica_groups=mesh['fsdp'=4,'ctx'=8] {'ctx'}, dimensions={1}, use_global_device_ids=true | all-gather | bytes 995328 | tf_op jit(solution)/shard_map/all_gather | solution.py:480
  638.6 1.3 bitcast_convert_fusion.2
  640.0 3.7 all-gather.38.cloned.1.call-done
  643.6 2.9 bitcast_convert_fusion.1
  646.6 20.7 %all-gather.40.cloned.1.call-done = bf16[1,768,768]{2,1,0:T(8,128)(2,1)} async-done(((bf16[1,96,768]{2,1,0:T(8,128)(2,1)}), bf16[1,768,768]{2,1,0:T(8,128)(2,1)}) %all-gather.40.cloned.1.call-update) | async-done | bytes 1179664 | tf_op jit(solution)/shard_map/all_gather | solution.py:480
  667.2 2.8 bitcast_convert_fusion
  (315 shorter events, 32.2 us)
Async XLA Ops:
  7.2 38.6 %all-gather.24.cloned.1.call-start = ((), (), s32[]{:S(2)}) async-start(), calls=%async_computation.20 | async-start | bytes 2211840 | tf_op jit(solution)/shard_map/all_gather | solution.py:459
  7.3 38.6 %copy-start.40 = (bf16[192,768]{1,0:T(8,128)(2,1)S(1)}, bf16[192,768]{1,0:T(8,128)(2,1)}, u32[]{:S(2)}) copy-start(bf16[192,768]{1,0:T(8,128)(2,1)} %param.24) | copy-start | bytes 884740
  9.3 76.4 %all-gather.30.cloned.1.call-start = ((), (), s32[]{:S(2)}) async-start(), calls=%async_computation.23 | async-start | bytes 2949120 | tf_op jit(solution)/shard_map/all_gather | solution.py:459
  10.2 115.4 %all-gather.34.cloned.1.call-start = ((), (), s32[]{:S(2)}) async-start(), calls=%async_computation.25 | async-start | bytes 2949120 | tf_op jit(solution)/shard_map/all_gather | solution.py:459
  11.1 74.6 %copy-start.60 = (bf16[768]{0:T(1024)(128)(2,1)S(1)}, bf16[768]{0:T(1024)(128)(2,1)}, u32[]{:S(2)}) copy-start(bf16[768]{0:T(1024)(128)(2,1)} %param.29) | copy-start | bytes 4612
  11.1 74.6 %copy-start.62 = (bf16[192]{0:T(256)(128)(2,1)S(1)}, bf16[192]{0:T(256)(128)(2,1)}, u32[]{:S(2)}) copy-start(bf16[192]{0:T(256)(128)(2,1)} %param.22) | copy-start | bytes 1156
  11.1 74.7 %copy-start.63 = (bf16[192]{0:T(256)(128)(2,1)S(1)}, bf16[192]{0:T(256)(128)(2,1)}, u32[]{:S(2)}) copy-start(bf16[192]{0:T(256)(128)(2,1)} %param.23) | copy-start | bytes 1156
  11.1 74.7 %copy-start.64 = (bf16[192]{0:T(256)(128)(2,1)S(1)}, bf16[192]{0:T(256)(128)(2,1)}, u32[]{:S(2)}) copy-start(bf16[192]{0:T(256)(128)(2,1)} %param.25) | copy-start | bytes 1156
  11.2 74.7 %copy-start.65 = (bf16[192]{0:T(256)(128)(2,1)S(1)}, bf16[192]{0:T(256)(128)(2,1)}, u32[]{:S(2)}) copy-start(bf16[192]{0:T(256)(128)(2,1)} %param.26) | copy-start | bytes 1156
  11.2 74.7 %copy-start.66 = (bf16[192]{0:T(256)(128)(2,1)S(1)}, bf16[192]{0:T(256)(128)(2,1)}, u32[]{:S(2)}) copy-start(bf16[192]{0:T(256)(128)(2,1)} %param.27) | copy-start | bytes 1156
  11.2 74.7 %copy-start.67 = (bf16[192]{0:T(256)(128)(2,1)S(1)}, bf16[192]{0:T(256)(128)(2,1)}, u32[]{:S(2)}) copy-start(bf16[192]{0:T(256)(128)(2,1)} %param.31) | copy-start | bytes 1156
  11.2 74.7 %copy-start.68 = (bf16[192]{0:T(256)(128)(2,1)S(1)}, bf16[192]{0:T(256)(128)(2,1)}, u32[]{:S(2)}) copy-start(bf16[192]{0:T(256)(128)(2,1)} %param.32) | copy-start | bytes 1156
  11.2 74.7 %copy-start.69 = (bf16[192]{0:T(256)(128)(2,1)S(1)}, bf16[192]{0:T(256)(128)(2,1)}, u32[]{:S(2)}) copy-start(bf16[192]{0:T(256)(128)(2,1)} %param.33) | copy-start | bytes 1156
  11.2 88.6 %copy-start.70 = (s32[16]{0:T(128)S(1)}, s32[16]{0:T(128)}, u32[]{:S(2)}) copy-start(s32[16]{0:T(128)} %param.20) | copy-start | bytes 196
  11.3 128.5 %all-gather.26.cloned.1.call-start = ((), (), s32[]{:S(2)}) async-start(), calls=%async_computation.21 | async-start | bytes 5308416 | tf_op jit(solution)/shard_map/all_gather | solution.py:460
  45.8 183.3 %all-gather.28.cloned.1.call-start = ((), (), s32[]{:S(2)}) async-start(), calls=%async_computation.22 | async-start | bytes 1769472 | tf_op jit(solution)/shard_map/all_gather | solution.py:460
  45.9 93.9 %copy-start.15 = (bf16[256,768]{1,0:T(8,128)(2,1)S(1)}, bf16[256,768]{1,0:T(8,128)(2,1)}, u32[]{:S(2)}) copy-start(bf16[256,768]{1,0:T(8,128)(2,1)} %param.17) | copy-start | bytes 1179652
  57.0 174.3 %all-gather.32.cloned.1.call-start = ((), (), s32[]{:S(2)}) async-start(), calls=%async_computation.24 | async-start | bytes 7077888 | tf_op jit(solution)/shard_map/all_gather | solution.py:460
  85.7 157.4 %all-gather.36.cloned.1.call-start = ((), (), s32[]{:S(2)}) async-start(), calls=%async_computation.26 | async-start | bytes 7077888 | tf_op jit(solution)/shard_map/all_gather | solution.py:460
  125.7 236.5 %reduce-scatter.29.cloned.1.call-start = ((), (), s32[]{:S(2)}) async-start(), calls=%async_computation.16 | async-start | bytes 7077888 | tf_op jit(solution)/shard_map/reduce_scatter | solution.py:473
  185.3 5.3 copy-start.61
  186.0 8.0 %copy-start.2 = (bf16[2,2048,128]{2,1,0:T(8,128)(2,1)}, bf16[2,2048,128]{2,1,0:T(8,128)(2,1)S(1)}, u32[]{:S(2)}) copy-start(bf16[2,2048,128]{2,1,0:T(8,128)(2,1)S(1)} %copy.89.key_ref) | copy-start | bytes 3145732
  190.9 16.1 %copy-start.4 = (bf16[3072,128]{1,0:T(8,128)(2,1)}, bf16[3072,128]{1,0:T(8,128)(2,1)S(1)}, u32[]{:S(2)}) copy-start(bf16[3072,128]{1,0:T(8,128)(2,1)S(1)} %maximum_maximum_fusion.query_ref) | copy-start | bytes 2359300
  207.0 21.4 %copy-start.3 = (f32[64,3072]{1,0:T(8,128)}, f32[64,3072]{1,0:T(8,128)S(1)}, u32[]{:S(2)}) copy-start(f32[64,3072]{1,0:T(8,128)S(1)} %get-tuple-element.20.out_ref) | copy-start | bytes 2359300
  207.7 21.5 %copy-start.49 = (f32[768]{0:T(1024)S(1)}, f32[768]{0:T(1024)}, u32[]{:S(2)}) copy-start(f32[768]{0:T(1024)} %reshape.391) | copy-start | bytes 9220
  231.0 12.1 %copy-start.42 = (f32[256]{0:T(256)}, f32[256]{0:T(256)S(1)}, u32[]{:S(2)}) copy-start(f32[256]{0:T(256)S(1)} %broadcast_multiply_fusion.2) | copy-start | bytes 3076
  231.2 11.9 %copy-start.54 = (f32[256]{0:T(256)}, f32[256]{0:T(256)S(1)}, u32[]{:S(2)}) copy-start(f32[256]{0:T(256)S(1)} %multiply_reduce_fusion.3) | copy-start | bytes 3076
  231.2 11.9 %copy-start.50 = (f32[256]{0:T(256)}, f32[256]{0:T(256)S(1)}, u32[]{:S(2)}) copy-start(f32[256]{0:T(256)S(1)} %fusion.48) | copy-start | bytes 3076
  231.3 11.8 %copy-start.56 = (f32[768]{0:T(1024)S(1)}, f32[768]{0:T(1024)}, u32[]{:S(2)}) copy-start(f32[768]{0:T(1024)} %reshape.395) | copy-start | bytes 9220
  243.1 7.6 %slice-start = ((s8[4718592]{0:T(1024)(128)(4,1)}), s8[4194304]{0:T(1024)(128)(4,1)S(1)}, s32[]{:S(2)}) async-start(s8[4718592]{0:T(1024)(128)(4,1)} %bitcast.296), calls=%async_computation.33 | async-start | bytes 8388608
  243.2 4.7 copy-start.17
  243.2 4.7 copy-start.41
  243.2 5.7 copy-start.48
  243.2 7.5 %slice-start.1 = ((s8[4718592]{0:T(1024)(128)(4,1)}), s8[524288]{0:T(1024)(128)(4,1)S(1)}, s32[]{:S(2)}) async-start(s8[4718592]{0:T(1024)(128)(4,1)} %bitcast.296), calls=%async_computation.34 | async-start | bytes 1048576
  243.2 7.5 %copy-start.72 = (f32[256,3072]{1,0:T(8,128)S(1)}, f32[256,3072]{1,0:T(8,128)}, u32[]{:S(2)}) copy-start(f32[256,3072]{1,0:T(8,128)} %get-tuple-element.172) | copy-start | bytes 9437188
  257.7 5.8 copy-start.55
  257.7 105.0 %reduce-scatter.25.cloned.1.call-start = ((), (), s32[]{:S(2)}) async-start(), calls=%async_computation.14 | async-start | bytes 1769472 | tf_op jit(solution)/shard_map/reduce_scatter | solution.py:473
  265.7 97.7 %reduce-scatter.33.cloned.1.call-start = ((), (), s32[]{:S(2)}) async-start(), calls=%async_computation.18 | async-start | bytes 7077888 | tf_op jit(solution)/shard_map/reduce_scatter | solution.py:473
  271.4 111.0 %reduce-scatter.21.cloned.1.call-start = ((), (), s32[]{:S(2)}) async-start(), calls=%async_computation.12 | async-start | bytes 5308416 | tf_op jit(solution)/shard_map/reduce_scatter | solution.py:473
  354.5 4.3 copy-start.19
  355.8 4.1 copy-start.29
  355.8 4.1 copy-start.31
  355.8 4.1 copy-start.32
  362.1 61.9 %reduce-scatter.41.cloned.1.call-start = ((), (), s32[]{:S(2)}) async-start(), calls=%async_computation.31 | async-start | bytes 2949120
  362.6 89.2 %reduce-scatter.39.cloned.1.call-start = ((), (), s32[]{:S(2)}) async-start(), calls=%async_computation.30 | async-start | bytes 737280
  363.4 189.1 %copy-start.20 = (bf16[256,64]{1,0:T(8,128)(2,1)S(1)}, bf16[256,64]{1,0:T(8,128)(2,1)}, u32[]{:S(2)}) copy-start(bf16[256,64]{1,0:T(8,128)(2,1)} %copy-done.19) | copy-start | bytes 98308
  363.4 129.1 %reduce-scatter.43.cloned.1.call-start = ((), (), s32[]{:S(2)}) async-start(), calls=%async_computation.32 | async-start | bytes 2949120
  363.5 190.2 %copy-start.22 = (bf16[256,64]{1,0:T(8,128)(2,1)S(1)}, bf16[256,64]{1,0:T(8,128)(2,1)}, u32[]{:S(2)}) copy-start(bf16[256,64]{1,0:T(8,128)(2,1)} %copy-done.21) | copy-start | bytes 98308
  363.5 190.2 %copy-start.24 = (bf16[256,64]{1,0:T(8,128)(2,1)S(1)}, bf16[256,64]{1,0:T(8,128)(2,1)}, u32[]{:S(2)}) copy-start(bf16[256,64]{1,0:T(8,128)(2,1)} %copy-done.23) | copy-start | bytes 98308
  363.5 190.2 %copy-start.26 = (bf16[256,64]{1,0:T(8,128)(2,1)S(1)}, bf16[256,64]{1,0:T(8,128)(2,1)}, u32[]{:S(2)}) copy-start(bf16[256,64]{1,0:T(8,128)(2,1)} %copy-done.25) | copy-start | bytes 98308
  363.5 190.2 %copy-start.28 = (bf16[256,64]{1,0:T(8,128)(2,1)S(1)}, bf16[256,64]{1,0:T(8,128)(2,1)}, u32[]{:S(2)}) copy-start(bf16[256,64]{1,0:T(8,128)(2,1)} %copy-done.27) | copy-start | bytes 98308
  363.5 190.2 %copy-start.30 = (bf16[256,64]{1,0:T(8,128)(2,1)S(1)}, bf16[256,64]{1,0:T(8,128)(2,1)}, u32[]{:S(2)}) copy-start(bf16[256,64]{1,0:T(8,128)(2,1)} %copy-done.29) | copy-start | bytes 98308
  364.0 164.2 %reduce-scatter.37.cloned.1.call-start = ((), (), s32[]{:S(2)}) async-start(), calls=%async_computation.29 | async-start | bytes 2211840
  382.4 175.1 %copy-start.47 = (f32[768]{0:T(1024)S(1)}, f32[768]{0:T(1024)}, u32[]{:S(2)}) copy-start(f32[768]{0:T(1024)} %get-tuple-element.31) | copy-start | bytes 9220
  382.4 175.1 %copy-start.46 = (f32[768]{0:T(1024)S(1)}, f32[768]{0:T(1024)}, u32[]{:S(2)}) copy-start(f32[768]{0:T(1024)} %get-tuple-element.27) | copy-start | bytes 9220
  382.4 175.2 %copy-start.45 = (f32[768]{0:T(1024)S(1)}, f32[768]{0:T(1024)}, u32[]{:S(2)}) copy-start(f32[768]{0:T(1024)} %get-tuple-element.30) | copy-start | bytes 9220
  382.4 216.2 %copy-start.12 = (f32[256,768]{1,0:T(8,128)S(1)}, f32[256,768]{1,0:T(8,128)}, u32[]{:S(2)}) copy-start(f32[256,768]{1,0:T(8,128)} %copy-done.11) | copy-start | bytes 2359300
  382.5 170.0 %reduce-scatter.31.cloned.1.call-start = ((), (), s32[]{:S(2)}) async-start(), calls=%async_computation.17 | async-start | bytes 737280 | tf_op jit(solution)/shard_map/reduce_scatter | solution.py:477
  423.9 178.6 %reduce-scatter.27.cloned.1.call-start = ((), (), s32[]{:S(2)}) async-start(), calls=%async_computation.15 | async-start | bytes 184320 | tf_op jit(solution)/shard_map/reduce_scatter | solution.py:477
  451.9 166.5 %reduce-scatter.35.cloned.1.call-start = ((), (), s32[]{:S(2)}) async-start(), calls=%async_computation.19 | async-start | bytes 737280 | tf_op jit(solution)/shard_map/reduce_scatter | solution.py:477
  492.5 126.8 %reduce-scatter.23.cloned.1.call-start = ((), (), s32[]{:S(2)}) async-start(), calls=%async_computation.13 | async-start | bytes 552960 | tf_op jit(solution)/shard_map/reduce_scatter | solution.py:477
  528.2 115.5 %all-gather.38.cloned.1.call-start = ((), (), s32[]{:S(2)}) async-start(), calls=%async_computation.27 | async-start | bytes 1327104 | tf_op jit(solution)/shard_map/all_gather | solution.py:480
  552.5 114.8 %all-gather.40.cloned.1.call-start = ((), (), s32[]{:S(2)}) async-start(), calls=%async_computation.28 | async-start | bytes 1327104 | tf_op jit(solution)/shard_map/all_gather | solution.py:480
  638.6 31.4 %copy-start.1 = (bf16[192,3072]{1,0:T(8,128)(2,1)S(1)}, bf16[192,3072]{1,0:T(8,128)(2,1)}, u32[]{:S(2)}) copy-start(bf16[192,3072]{1,0:T(8,128)(2,1)} %param.28) | copy-start | bytes 3538948
  (32 other events, 79.1 us)
Sparse Core Ops, SparseCore 0:
  10.5 35.2 all-gather.23
  48.2 37.4 all-gather.29
  88.1 37.4 all-gather.33
  127.0 12.6 all-gather.25
  141.2 10.3 all-gather.27
  153.0 15.5 all-gather.31
  170.2 15.6 all-gather.35
  257.8 15.8 reduce-scatter.28
  276.0 9.8 reduce-scatter.24
  288.0 13.7 reduce-scatter.32
  362.2 20.1 reduce-scatter.20
  385.3 38.5 reduce-scatter.40
  426.8 25.0 reduce-scatter.38
  455.1 37.3 reduce-scatter.42
  495.6 32.4 reduce-scatter.36
  530.4 21.9 reduce-scatter.30
  554.6 17.6 reduce-scatter.26
  574.4 20.1 reduce-scatter.34
  596.9 20.2 reduce-scatter.22
  618.7 24.8 all-gather.37
  645.4 21.8 all-gather.39

commit v2 on v1

--- a/solution.py
+++ b/solution.py
@@ -58,61 +58,383 @@
     return jnp.exp(scores - lse_blk[:, :, None])
 
 
-def exchange_kernel(n, axis, x_ref, y_ref, send_sem, recv_sem, own_sem):
-    me = lax.axis_index(axis)
+MESH_IDS = pl.DeviceIdType.MESH
+
+
+def beside():
+    f = lax.axis_index("fsdp")
+    c = lax.axis_index("ctx")
+    x, y = lax.rem(f, 2), f // 2
+    core = lax.rem(c, 2)
+    over_x = 2 * y + (1 - x)
+    over_y = 2 * (1 - y) + x
+    over_both = 2 * (1 - y) + (1 - x)
+    return f, over_x, over_y, over_both, core, c + 1 - 2 * core
+
+
+def greet(targets):
     barrier = pltpu.get_barrier_semaphore()
-    for step in range(1, n):
-        pl.semaphore_signal(
-            barrier,
-            inc=1,
-            device_id={axis: lax.rem(me + step, n)},
-            device_id_type=pl.DeviceIdType.MESH,
-        )
-    own = pltpu.make_async_copy(x_ref.at[me], y_ref.at[me], own_sem)
-    own.start()
-    pl.semaphore_wait(barrier, n - 1)
-    for step in range(1, n):
-        peer = lax.rem(me + step, n)
-        pltpu.make_async_remote_copy(
-            src_ref=x_ref.at[peer],
-            dst_ref=y_ref.at[me],
-            send_sem=send_sem.at[step],
-            recv_sem=recv_sem.at[step],
-            device_id={axis: peer},
-            device_id_type=pl.DeviceIdType.MESH,
-        ).start()
-    own.wait()
-    for step in range(1, n):
-        source = lax.rem(me + n - step, n)
-        copy = pltpu.make_async_remote_copy(
-            src_ref=x_ref.at[source],
-            dst_ref=y_ref.at[source],
-            send_sem=send_sem.at[step],
-            recv_sem=recv_sem.at[step],
-            device_id={axis: source},
-            device_id_type=pl.DeviceIdType.MESH,
-        )
-        copy.wait()
-
-
-def exchange(blocks, axis, number):
+    for target in targets:
+        pl.semaphore_signal(barrier, inc=1, device_id=target, device_id_type=MESH_IDS)
+    pl.semaphore_wait(barrier, len(targets))
+
+
+def remote(source, target, send, recv, device):
+    return pltpu.make_async_remote_copy(
+        src_ref=source,
+        dst_ref=target,
+        send_sem=send,
+        recv_sem=recv,
+        device_id=device,
+        device_id_type=MESH_IDS,
+    )
+
+
+class Swap:
+    def __init__(self, n, x_ref, y_ref, send_sem, recv_sem, own_sem):
+        self.n, self.x_ref, self.y_ref = n, x_ref, y_ref
+        self.send_sem, self.recv_sem, self.own_sem = send_sem, recv_sem, own_sem
+        self.me = lax.axis_index("ctx")
+        self.own = pltpu.make_async_copy(x_ref.at[self.me], y_ref.at[self.me], own_sem)
+
+    def targets(self):
+        return [{"ctx": lax.rem(self.me + step, self.n)} for step in range(1, self.n)]
+
+    def start(self):
+        self.own.start()
+        for step in range(1, self.n):
+            peer = lax.rem(self.me + step, self.n)
+            remote(
+                self.x_ref.at[peer],
+                self.y_ref.at[self.me],
+                self.send_sem.at[step],
+                self.recv_sem.at[step],
+                {"ctx": peer},
+            ).start()
+
+    def finish(self):
+        self.own.wait()
+        for step in range(1, self.n):
+            source = lax.rem(self.me + self.n - step, self.n)
+            remote(
+                self.x_ref.at[source],
+                self.y_ref.at[source],
+                self.send_sem.at[step],
+                self.recv_sem.at[step],
+                {"ctx": source},
+            ).wait()
+
+
+class Gather:
+    def __init__(self, w_ref, o_ref, send_sem, recv_sem, own_sem):
+        self.w_ref, self.o_ref = w_ref, o_ref
+        self.f, self.fx, self.fy, self.fd, self.core, self.sibling = beside()
+        half = w_ref.shape[1] // 2
+        upper, lower = pl.ds(0, half), pl.ds(half, half)
+        f, fx, fy, fd, k = self.f, self.fx, self.fy, self.fd, self.core
+        to_x, to_y, to_core = {"fsdp": fx}, {"fsdp": fy}, {"ctx": self.sibling}
+        o = o_ref
+
+        def copy(number, source, target, device):
+            return remote(source, target, send_sem.at[number], recv_sem.at[number], device)
+
+        self.own = pltpu.make_async_copy(w_ref, o.at[f], own_sem)
+        self.sends = [
+            copy(0, w_ref.at[k], o.at[f, k], to_x),
+            copy(1, w_ref.at[k], o.at[f, k], to_y),
+            copy(2, o.at[fx, k, upper], o.at[fx, k, upper], to_y),
+            copy(3, o.at[fx, k], o.at[fx, k], to_core),
+            copy(4, o.at[fy, k, lower], o.at[fy, k, lower], to_x),
+            copy(5, o.at[fy, k], o.at[fy, k], to_core),
+            copy(6, o.at[fd, k], o.at[fd, k], to_core),
+        ]
+        other = 1 - k
+        self.takes = [
+            copy(0, w_ref.at[k], o.at[fx, k], to_x),
+            copy(1, w_ref.at[k], o.at[fy, k], to_y),
+            copy(2, o.at[fd, k, upper], o.at[fd, k, upper], to_y),
+            copy(3, o.at[fx, other], o.at[fx, other], to_core),
+            copy(4, o.at[fd, k, lower], o.at[fd, k, lower], to_x),
+            copy(5, o.at[fy, other], o.at[fy, other], to_core),
+            copy(6, o.at[fd, other], o.at[fd, other], to_core),
+        ]
+
+    def targets(self):
+        return [{"fsdp": self.fx}, {"fsdp": self.fy}]
+
+    def start(self):
+        self.sends[0].start()
+        self.sends[1].start()
+        self.own.start()
+
+    def finish(self):
+        self.takes[0].wait_recv()
+        self.sends[2].start()
+        self.sends[3].start()
+        self.takes[1].wait_recv()
+        self.sends[4].start()
+        self.sends[5].start()
+        self.takes[2].wait_recv()
+        self.takes[4].wait_recv()
+        self.sends[6].start()
+        for number in (3, 5, 6):
+            self.takes[number].wait_recv()
+        self.own.wait()
+        for send in self.sends:
+            send.wait_send()
+
+
+def swap_kernel(n, x_ref, y_ref, *sems):
+    swap = Swap(n, x_ref, y_ref, *sems)
+    greet(swap.targets())
+    swap.start()
+    swap.finish()
+
+
+def gather_kernel(w_ref, o_ref, *sems):
+    gather = Gather(w_ref, o_ref, *sems)
+    greet(gather.targets() + [{"ctx": gather.sibling}])
+    gather.start()
+    gather.finish()
+
+
+def swap_gather_kernel(n, x_ref, w_ref, y_ref, o_ref, *sems):
+    swap = Swap(n, x_ref, y_ref, *sems[:3])
+    gather = Gather(w_ref, o_ref, *sems[3:])
+    greet(swap.targets() + gather.targets())
+    gather.start()
+    swap.start()
+    gather.finish()
+    swap.finish()
+
+
+def vmem_specs(count):
+    return [pl.BlockSpec(memory_space=pltpu.VMEM)] * count
+
+
+def copy_sems(count):
+    return [
+        pltpu.SemaphoreType.DMA((count,)),
+        pltpu.SemaphoreType.DMA((count,)),
+        pltpu.SemaphoreType.DMA,
+    ]
+
+
+def linked(number, limit):
+    return pltpu.CompilerParams(
+        collective_id=number, has_side_effects=True, vmem_limit_bytes=limit << 20
+    )
+
+
+def exchange(blocks, number):
     n = blocks.shape[0]
-    size = 2 * blocks.size * blocks.dtype.itemsize
     return pl.pallas_call(
-        functools.partial(exchange_kernel, n, axis),
+        functools.partial(swap_kernel, n),
         out_shape=jax.ShapeDtypeStruct(blocks.shape, blocks.dtype),
-        in_specs=[pl.BlockSpec(memory_space=pltpu.VMEM)],
-        out_specs=pl.BlockSpec(memory_space=pltpu.VMEM),
+        in_specs=vmem_specs(1),
+        out_specs=vmem_specs(1)[0],
+        scratch_shapes=copy_sems(n),
+        compiler_params=linked(number, 16),
+    )(blocks)
+
+
+def gather_kernel_call(shard, number):
+    rows, columns = shard.shape
+    whole = pl.pallas_call(
+        gather_kernel,
+        out_shape=jax.ShapeDtypeStruct((4, 2, rows // 2, columns), shard.dtype),
+        in_specs=vmem_specs(1),
+        out_specs=vmem_specs(1)[0],
+        scratch_shapes=copy_sems(7),
+        compiler_params=linked(number, 16),
+    )(shard.reshape(2, rows // 2, columns))
+    return whole.reshape(4 * rows, columns)
+
+
+def exchange_gather(blocks, shard, number):
+    n = blocks.shape[0]
+    rows, columns = shard.shape
+    swapped, whole = pl.pallas_call(
+        functools.partial(swap_gather_kernel, n),
+        out_shape=[
+            jax.ShapeDtypeStruct(blocks.shape, blocks.dtype),
+            jax.ShapeDtypeStruct((4, 2, rows // 2, columns), shard.dtype),
+        ],
+        in_specs=vmem_specs(2),
+        out_specs=vmem_specs(2),
+        scratch_shapes=copy_sems(n) + copy_sems(7),
+        compiler_params=linked(number, 24),
+    )(blocks, shard.reshape(2, rows // 2, columns))
+    return swapped, whole.reshape(4 * rows, columns)
+
+
+CHUNKS = 3
+
+
+def wide_sum(*parts):
+    total = parts[0].astype(jnp.float32)
+    for part in parts[1:]:
+        total = total + part.astype(jnp.float32)
+    return total.astype(jnp.bfloat16)
+
+
+def reduce_kernel(*refs):
+    ins, outs = refs[:CHUNKS], refs[CHUNKS : 2 * CHUNKS]
+    halves, side, turn, deep, send_sem, recv_sem = refs[2 * CHUNKS :]
+    f, fx, fy, _, k, sibling = beside()
+    c = lax.axis_index("ctx")
+    z = c // 2
+    x, y = lax.rem(f, 2), f // 2
+    to_x, to_y, to_core = {"fsdp": fx}, {"fsdp": fy}, {"ctx": sibling}
+    depth = [lax.rem(z + step, 4) for step in range(1, 4)]
+    source = [lax.rem(z + 4 - step, 4) for step in range(1, 4)]
+    to_z = [{"ctx": 2 * peer + k} for peer in depth]
+    low, high = pl.ds(0, 2), pl.ds(2, 2)
+
+    def copy(j, number, origin, target, device):
+        return remote(origin, target, send_sem.at[j, number], recv_sem.at[j, number], device)
+
+    def core_copies(j):
+        return [
+            copy(j, g, ins[j].at[g, 1 - k], halves.at[j, g], to_core) for g in range(4)
+        ]
+
+    def side_copies(j):
+        copies = []
+        for t in range(2):
+            goes = 2 * t + (1 - x)
+            copies.append(copy(j, 4 + t, halves.at[j, goes, low], side.at[j, t], to_x))
+            goes = 2 * (1 - y) + t
+            copies.append(copy(j, 6 + t, halves.at[j, goes, high], side.at[j, 2 + t], to_y))
+        return copies
+
+    def turn_copies(j):
+        return [
+            copy(j, 8, halves.at[j, fy, low], turn.at[j, 0], to_y),
+            copy(j, 9, halves.at[j, fx, high], turn.at[j, 1], to_x),
+        ]
+
+    def deep_copies(j):
+        return [
+            copy(j, 10 + i, halves.at[j, f, depth[i]], deep.at[j, i], to_z[i]) for i in range(3)
+        ]
+
+    def back_copies(j):
+        return [copy(j, 13 + i, outs[j].at[k, z], outs[j].at[k, z], to_z[i]) for i in range(3)]
+
+    def back_takes(j):
+        return [
+            copy(j, 13 + i, outs[j].at[k, source[i]], outs[j].at[k, source[i]], to_z[i])
+            for i in range(3)
+        ]
+
+    def last_copy(j):
+        return copy(j, 16, outs[j].at[k], outs[j].at[k], to_core)
+
+    def last_take(j):
+        return copy(j, 16, outs[j].at[1 - k], outs[j].at[1 - k], to_core)
+
+    def start_all(copies):
+        for one in copies:
+            one.start()
+
+    def take_all(copies):
+        for one in copies:
+            one.wait_recv()
+
+    def phase_core(j):
+        take_all(core_copies(j))
+
+        @pl.loop(0, 16)
+        def _(i):
+            g, d = i // 4, lax.rem(i, 4)
+            halves[j, g, d] = wide_sum(halves[j, g, d], ins[j][g, k, d])
+
+        start_all(side_copies(j))
+
+    def phase_side(j):
+        copies = side_copies(j)
+        for one in copies:
+            one.wait()
+
+        @pl.loop(0, 2)
+        def _(d):
+            for t in range(2):
+                keeps = 2 * t + x
+                halves[j, keeps, d] = wide_sum(halves[j, keeps, d], side[j, t, d])
+                keeps = 2 * y + t
+                halves[j, keeps, 2 + d] = wide_sum(halves[j, keeps, 2 + d], side[j, 2 + t, d])
+
+        start_all(turn_copies(j))
+
+    def phase_turn(j):
+        for one in turn_copies(j):
+            one.wait()
+
+        @pl.loop(0, 2)
+        def _(d):
+            halves[j, f, d] = wide_sum(halves[j, f, d], turn[j, 0, d])
+            halves[j, f, 2 + d] = wide_sum(halves[j, f, 2 + d], turn[j, 1, d])
+
+        start_all(deep_copies(j))
+
+    def phase_deep(j):
+        take_all(deep_copies(j))
+        outs[j][k, z] = wide_sum(halves[j, f, z], deep[j, 0], deep[j, 1], deep[j, 2])
+        start_all(back_copies(j))
+
+    def phase_back(j):
+        take_all(back_takes(j))
+        last_copy(j).start()
+
+    def phase_last(j):
+        last_take(j).wait_recv()
+        for one in core_copies(j) + deep_copies(j) + back_copies(j) + [last_copy(j)]:
+            one.wait_send()
+
+    greet([to_x, to_y, to_core] + to_z)
+    for j in range(CHUNKS):
+        start_all(core_copies(j))
+    phases = [phase_core, phase_side, phase_turn, phase_deep, phase_back, phase_last]
+    for tick in range(CHUNKS + len(phases) - 1):
+        for order in reversed(range(len(phases))):
+            if 0 <= tick - order < CHUNKS:
+                phases[order](tick - order)
+
+
+def reduce_grads(chunks):
+    count, rows, width = chunks[0].shape
+    piece = rows // 8
+    shaped = [chunk.reshape(4, 2, 4, piece, width) for chunk in chunks]
+    low = jnp.bfloat16
+    outs = pl.pallas_call(
+        reduce_kernel,
+        out_shape=[jax.ShapeDtypeStruct((2, 4, piece, width), low)] * CHUNKS,
+        in_specs=vmem_specs(CHUNKS),
+        out_specs=vmem_specs(CHUNKS),
         scratch_shapes=[
-            pltpu.SemaphoreType.DMA((n,)),
-            pltpu.SemaphoreType.DMA((n,)),
-            pltpu.SemaphoreType.DMA,
+            pltpu.VMEM((CHUNKS, 4, 4, piece, width), low),
+            pltpu.VMEM((CHUNKS, 4, 2, piece, width), low),
+            pltpu.VMEM((CHUNKS, 2, 2, piece, width), low),
+            pltpu.VMEM((CHUNKS, 3, piece, width), low),
+            pltpu.SemaphoreType.DMA((CHUNKS, 17)),
+            pltpu.SemaphoreType.DMA((CHUNKS, 17)),
         ],
-        compiler_params=pltpu.CompilerParams(
-            collective_id=number, has_side_effects=True, vmem_limit_bytes=size + (4 << 20)
-        ),
-        cost_estimate=pl.CostEstimate(flops=0, bytes_accessed=10 * size, transcendentals=0),
-    )(blocks)
+        compiler_params=linked(6, 48),
+    )(*shaped)
+    return [out.reshape(rows, width).astype(jnp.float32) for out in outs]
+
+
+def split_wide(grad):
+    rows, columns = grad.shape
+    feat_width = HEADS * HEAD_DIM
+    parts = grad.reshape(4, rows // 4, columns // feat_width, feat_width)
+    return jnp.swapaxes(parts, 1, 2).reshape(4, -1, feat_width)
+
+
+def join_wide(shard, rows):
+    parts = shard.reshape(-1, rows, shard.shape[1])
+    return jnp.swapaxes(parts, 0, 1).reshape(rows, -1)
 
 
 QTILE = 512
@@ -236,7 +558,7 @@
     return 3 * (target // 2) + target % 2, 3 * (target // 2) + 2
 
 
-def dealt_forward(packed, block_table, seq_length, n_ctx):
+def dealt_forward(packed, block_table, seq_length, n_ctx, inner_weight, outer_weight):
     rows = packed.shape[0]
     half = n_ctx // 2 * rows
     core = lax.axis_index("ctx") % 2
@@ -249,7 +571,8 @@
                 [whole, HEADS + whole, 2 * HEADS + whole, shared, HEADS + shared, 2 * HEADS + shared],
             )
         )
-    got = exchange(jnp.stack(sends), "ctx", 1).reshape(n_ctx * rows, 6, HEAD_DIM)
+    got, inner_full = exchange_gather(jnp.stack(sends), inner_weight, 1)
+    got = got.reshape(n_ctx * rows, 6, HEAD_DIM)
     total = n_ctx * rows
     valid = key_valid(0, total, BLK, block_table, seq_length)
     mask_col = jnp.where(valid, 0.0, NEG_FILL).astype(jnp.bfloat16)[:, None]
@@ -274,7 +597,9 @@
     second = lax.dynamic_update_slice_in_dim(
         jnp.zeros((total, HEAD_DIM), jnp.bfloat16), low[total:], core * half, axis=0
     ).reshape(n_ctx, rows, HEAD_DIM)
-    back = exchange(jnp.concatenate([first, second], axis=2), "ctx", 2)
+    back, outer_full = exchange_gather(
+        jnp.concatenate([first, second], axis=2), outer_weight, 2
+    )
     upper = lax.axis_index("ctx") >= n_ctx // 2
     pieces = []
     for chip in range(n_ctx // 2):
@@ -283,7 +608,8 @@
             back[2 * chip + 1, :, :HEAD_DIM],
             jnp.where(upper, back[2 * chip + 1, :, HEAD_DIM:], back[2 * chip, :, HEAD_DIM:]),
         ]
-    return jnp.concatenate(pieces, axis=1), (query, key, value, out, lse)
+    context = jnp.concatenate(pieces, axis=1)
+    return context, (query, key, value, out, lse), inner_full, outer_full
 
 
 def dealt_backward(context_grad, saved, n_ctx):
@@ -293,7 +619,7 @@
     half = total // 2
     core = lax.axis_index("ctx") % 2
     sends = jnp.stack([pick_heads(context_grad, unit_heads(target)) for target in range(n_ctx)])
-    got = exchange(sends, "ctx", 3).reshape(total, 2 * HEAD_DIM)
+    got = exchange(sends, 3).reshape(total, 2 * HEAD_DIM)
     grad = jnp.concatenate(
         [
             got[:, :HEAD_DIM],
@@ -314,7 +640,7 @@
     sends = jnp.concatenate(
         [dquery[:total], dkey[0], dvalue[0], dshared, dkey[1], dvalue[1]], axis=1
     ).reshape(n_ctx, rows, 6 * HEAD_DIM)
-    back = exchange(sends, "ctx", 4)
+    back = exchange(sends, 4)
     piece = lambda source, k: back[source, :, k * HEAD_DIM : (k + 1) * HEAD_DIM]
     both = lambda chip, k: (
         piece(2 * chip, k).astype(jnp.float32) + piece(2 * chip + 1, k).astype(jnp.float32)
@@ -443,42 +769,11 @@
     return jnp.concatenate([query_grad, key_grad, value_grad], axis=1).astype(jnp.bfloat16)
 
 
-def core_pairs(n_ctx):
-    return [[2 * z, 2 * z + 1] for z in range(n_ctx // 2)]
-
-
-def core_columns(n_ctx):
-    return [list(range(0, n_ctx, 2)), list(range(1, n_ctx, 2))]
-
-
-def gather_weight(shard, n_ctx):
-    rows, columns = shard.shape
-    half = rows // 2
-    core = lax.axis_index("ctx") % 2
-    mine = lax.dynamic_slice_in_dim(shard, core * half, half, axis=0)
-    quarter = lax.all_gather(mine, "fsdp", axis=0)
-    whole = lax.all_gather(quarter, "ctx", axis=1, axis_index_groups=core_pairs(n_ctx))
-    return whole.reshape(-1, columns)
-
-
-def reduce_weight(grad, n_fsdp, n_ctx):
-    rows, columns = grad.shape
-    if n_ctx != 8:
-        part = lax.psum_scatter(
-            grad.astype(jnp.bfloat16), "fsdp", scatter_dimension=0, tiled=True
-        ).astype(jnp.float32)
-        return lax.psum(part, "ctx")
-    piece = rows // (n_fsdp * n_ctx)
-    low = grad.astype(jnp.bfloat16).reshape(n_fsdp, n_ctx // 2, 2, piece, columns)
-    low = lax.psum_scatter(
-        low, "ctx", scatter_dimension=2, axis_index_groups=core_pairs(n_ctx)
-    )
-    low = lax.psum_scatter(low, "fsdp", scatter_dimension=0)
-    low = lax.psum_scatter(
-        low, "ctx", scatter_dimension=0, axis_index_groups=core_columns(n_ctx)
-    )
-    whole = lax.all_gather(low, "ctx", axis=0, tiled=True)
-    return whole.astype(jnp.float32)
+def reduce_weight(grad):
+    part = lax.psum_scatter(
+        grad.astype(jnp.bfloat16), "fsdp", scatter_dimension=0, tiled=True
+    ).astype(jnp.float32)
+    return lax.psum(part, "ctx")
 
 
 def local(
@@ -505,7 +800,7 @@
     seq_length = lengths[0]
     n_fsdp = lax.axis_size("fsdp")
     n_ctx = lax.axis_size("ctx")
-    dealt = n_ctx == 8 and tok_rows == 256
+    dealt = n_ctx == 8 and n_fsdp == 4 and tok_rows == 256
     vectors = (
         query_bias,
         value_bias,
@@ -532,10 +827,15 @@
         gain2_full,
         shift2_full,
     ) = [gathered[:, ends[k] : ends[k + 1]].reshape(-1) for k in range(len(vectors))]
-    qkv_full = gather_weight(qkv_weight, n_ctx)
-    proj_full = gather_weight(proj_weight, n_ctx)
-    inner_full = gather_weight(inner_weight, n_ctx)
-    outer_full = gather_weight(outer_weight, n_ctx)
+    if dealt:
+        both_full = gather_kernel_call(jnp.concatenate([qkv_weight, proj_weight], axis=1), 5)
+        qkv_full = both_full[:, : 3 * feat_width]
+        proj_full = both_full[:, 3 * feat_width :]
+    else:
+        qkv_full, proj_full, inner_full, outer_full = [
+            lax.all_gather(weight, "fsdp", axis=0, tiled=True)
+            for weight in (qkv_weight, proj_weight, inner_weight, outer_weight)
+        ]
     tokens_wide = tokens.astype(jnp.float32)
     bias_row = jnp.concatenate([qbias_full, jnp.zeros_like(qbias_full), vbias_full]).astype(
         jnp.float32
@@ -544,7 +844,9 @@
         jnp.bfloat16
     )
     if dealt:
-        context, saved = dealt_forward(packed, block_table, seq_length, n_ctx)
+        context, saved, inner_full, outer_full = dealt_forward(
+            packed, block_table, seq_length, n_ctx, inner_weight, outer_weight
+        )
     else:
         context, saved = scan_forward(packed, block_table, seq_length)
     hidden = (
@@ -607,19 +909,42 @@
     bundle = lax.psum(bundle, ("fsdp", "ctx"))
     bundle = lax.dynamic_index_in_dim(bundle, lax.axis_index("fsdp"), axis=0, keepdims=False)
     vector_parts = [bundle[ends[k] : ends[k + 1]] for k in range(len(sums))]
+    if dealt:
+        low = jnp.bfloat16
+        inner_sum, outer_sum, attn_sum = reduce_grads(
+            [
+                split_wide(inner_grad.astype(low)),
+                outer_grad.astype(low).reshape(4, feat_width, feat_width),
+                jnp.concatenate(
+                    [
+                        split_wide(qkv_grad.astype(low)),
+                        proj_grad.astype(low).reshape(4, feat_width // 4, feat_width),
+                    ],
+                    axis=1,
+                ),
+            ]
+        )
+        shard_rows = feat_width // 4
+        inner_sum = join_wide(inner_sum, shard_rows)
+        qkv_sum = join_wide(attn_sum[: 3 * shard_rows], shard_rows)
+        proj_sum = attn_sum[3 * shard_rows :]
+    else:
+        qkv_sum, proj_sum, inner_sum, outer_sum = [
+            reduce_weight(grad) for grad in (qkv_grad, proj_grad, inner_grad, outer_grad)
+        ]
     return (
         layer_out,
         tokens_grad,
-        reduce_weight(qkv_grad, n_fsdp, n_ctx),
+        qkv_sum,
         vector_parts[0],
         vector_parts[1],
-        reduce_weight(proj_grad, n_fsdp, n_ctx),
+        proj_sum,
         vector_parts[2],
         vector_parts[3],
         vector_parts[4],
-        reduce_weight(inner_grad, n_fsdp, n_ctx),
+        inner_sum,
         vector_parts[5],
-        reduce_weight(outer_grad, n_fsdp, n_ctx),
+        outer_sum,
         vector_parts[6],
         vector_parts[7],
         vector_parts[8],

time: 682 us -> 527 us (0.77)
  waiting for transfers between devices: 317 us -> 0 us
  Pallas kernels: 130 us -> 288 us
  local copies, waits for them, and re-layouts: 60.7 us -> 109 us
  blocking collectives: 93.9 us -> 51.2 us
  between operations: 17 us -> 2.98 us
    pallas_call x4 -> x6, Pallas kernels: 96.2 us -> 255 us  [the longest x1 122 us: reduce_grads(): pl.pallas_call(reduce_kernel, out_shape=[jax.ShapeDtypeStruct((2, 4, piec...]
    unnamed x25 -> x0, waiting for transfers between devices: 147 us -> none
    all_gather x9 -> x0, waiting for transfers between devices: 127 us -> none  [the longest x3 88.9 us: gather_weight(): quarter = lax.all_gather(mine, 'fsdp', axis=0)]
    all_gather x3 -> x0, blocking collectives: 46.3 us -> none  [the longest x2 35.2 us: reduce_weight(): whole = lax.all_gather(low, 'ctx', axis=0, tiled=True)]
    reduce_scatter x8 -> x0, waiting for transfers between devices: 42.7 us -> none  [the longest x4 24.2 us: reduce_weight(): lax.psum_scatter(low, 'ctx', scatter_dimension=0, axis_index_groups=core_...]
    reshape x5 -> x6, local copies, waits for them, and re-layouts: 9.7 us -> 29.6 us  [the longest x3 24.2 us: split_wide(): parts = grad.reshape(4, rows // 4, columns // feat_width, feat_width)]
    unnamed x167 -> x138, local copies, waits for them, and re-layouts: 8.26 us -> 15.4 us
  transfers between devices with their start and end apart: 21 -> 0, of which waited for: 12 -> 0; matrix products, arithmetic and copies ran while one was open for 14% -> 0% of each run, Pallas kernels for 19% -> 0%
where the time goes in v2:
time: 527 us; the launch traced here: 518 us
  Pallas kernels  288 us (55%)
  local copies, waits for them, and re-layouts  109 us (21%)
  blocking collectives  51.2 us (10%)
  matrix products  43.2 us (8%)
  other arithmetic  23.6 us (4%)
    pallas_call x1, Pallas kernels, reduce_grads(): pl.pallas_call(reduce_kernel, out_shape=[jax.ShapeDtypeStruct((2, 4, piec...  122 us
    pallas_call x2, Pallas kernels, exchange_gather(): pl.pallas_call(functools.partial(swap_gather_kernel, n), out_shape=[jax.S...  65.9 us
    pallas_call x2, Pallas kernels, exchange(): pl.pallas_call(functools.partial(swap_kernel, n), out_shape=jax.ShapeDtyp...  43.4 us
    psum x1, blocking collectives, local(): bundle = lax.psum(bundle, ('fsdp', 'ctx'))  41.5 us
    reshape x3, local copies, waits for them, and re-layouts, split_wide(): parts = grad.reshape(4, rows // 4, columns // feat_width, feat_width)  24.2 us
    pallas_call x1, Pallas kernels, gather_kernel_call(): pl.pallas_call(gather_kernel, out_shape=jax.ShapeDtypeStruct((4, 2, rows...  23.6 us
    pallas_call x1, Pallas kernels, attend_back(): pl.pallas_call(functools.partial(attend_back_kernel, tiles_first), grid=(...  20.4 us
    unnamed x138, local copies, waits for them, and re-layouts  15.4 us

profile of v2, /device:TPU:0, one launch (start us, length us, event | category | flops | bytes accessed | tf_op | source)
XLA Modules:
  0.0 518.3 jit_solution(5436112625564628320)
XLA Ops:
  0.6 6.1 %concatenate.120 = bf16[2304]{0:T(1024)(128)(2,1)S(1)} concatenate(bf16[192]{0:T(256)(128)(2,1)} %param.22, bf16[192]{0:T(256)(128)(2,1)} %param.23, bf16[192]{0:T(256)(128)(2,1)} %param.25, bf16[192]{0:T(256)(128)(2,1)} %param.26, bf16[192]{0:T(256)(128)(2,1)} %param.27, bf16[768]{0:T(1024)(128)(2,1)} %param.29, bf16[192]{0:T(256)(128)(2,1)} %param.31, bf16[192]{0:T(256)(128)(2,1)} %param.32, ...), dimensions={0} | concatenate | bytes 9216 | tf_op jit(solution)/shard_map/concatenate | solution.py:818
  6.8 9.6 %all-gather.1 = bf16[4,1,2304]{2,1,0:T(2,128)(2,1)S(1)} all-gather(bf16[1,1,2304]{2,1,0:T(2,128)(2,1)S(1)} %reshape.445), channel_id=2, replica_groups=mesh['fsdp'=4,'ctx'=8] {'fsdp'}, dimensions={0}, use_global_device_ids=true | all-gather | bytes 23040 | tf_op jit(solution)/shard_map/all_gather | solution.py:818
  18.4 1.4 pad_maximum_fusion.2
  19.8 23.6 %shard_map.280 = bf16[4,2,96,3072]{3,2,1,0:T(8,128)(2,1)S(1)} custom-call(bf16[2,96,3072]{2,1,0:T(8,128)(2,1)S(1)} %bitcast.249), custom_call_target="tpu_custom_call" | custom-call | tf_op jit(solution)/shard_map/pallas_call | solution.py:243
  43.5 2.1 copy-done
  45.8 3.1 fusion.2
  50.1 1.1 concatenate.125
  52.3 1.1 fusion.69
  58.1 1.3 copy-done.2
  59.3 30.3 %shard_map.281 = (bf16[8,256,384]{2,1,0:T(8,128)(2,1)S(1)}, bf16[4,2,96,3072]{3,2,1,0:T(8,128)(2,1)S(1)}) custom-call(bf16[8,256,384]{2,1,0:T(8,128)(2,1)S(1)} %bitcast_dynamic-update-slice_fusion.x_ref, bf16[2,96,3072]{2,1,0:T(8,128)(2,1)S(1)} %bitcast.252), custom_call_target="tpu_custom_call" | custom-call | tf_op jit(solution)/shard_map/pallas_call | solution.py:257
  89.6 2.2 copy-done.6
  91.9 2.0 copy.105
  93.8 2.6 reshape.405
  99.8 1.1 pad_maximum_fusion.1
  100.8 1.6 copy.110.key_ref
  103.0 1.6 pad_maximum_fusion.3
  104.6 1.5 copy.111.value_ref
  106.2 12.9 %shard_map.282 = (f32[64,3072]{1,0:T(8,128)S(1)}, f32[1,3072]{1,0:T(1,128)S(1)}) custom-call(bf16[3072,128]{1,0:T(8,128)(2,1)S(1)} %maximum_maximum_fusion.query_ref, bf16[2,2048,128]{2,1,0:T(8,128)(2,1)S(1)} %copy.110.key_ref, bf16[2,64,2048]{2,1,0:T(8,128)(2,1)S(1)} %copy.111.value_ref), custom_call_target="tpu_custom_call" | custom-call | flops 1610612736 | bytes 8388608 | tf_op jit(solution)/shard_map/pallas_call | solution.py:458
  120.6 1.4 pad_maximum_fusion.6.x_ref
  122.0 35.7 %shard_map.283 = (bf16[8,256,128]{2,1,0:T(8,128)(2,1)S(1)}, bf16[4,2,384,768]{3,2,1,0:T(8,128)(2,1)S(1)}) custom-call(bf16[8,256,128]{2,1,0:T(8,128)(2,1)S(1)} %pad_maximum_fusion.6.x_ref, bf16[2,384,768]{2,1,0:T(8,128)(2,1)S(1)} %bitcast.251), custom_call_target="tpu_custom_call" | custom-call | tf_op jit(solution)/shard_map/pallas_call | solution.py:257
  157.7 2.2 copy-done.7
  160.6 2.0 fusion.76
  163.0 11.7 %multiply_convert_fusion = (bf16[256,3072]{1,0:T(8,128)(2,1)S(1)}, f32[256,3072]{1,0:T(8,128)}, f32[256,3072]{1,0:T(8,128)}) fusion(f32[3072]{0:T(1024)S(1)} %copy-done.48, bf16[768,3072]{1,0:T(8,128)(2,1)} %bitcast.253, f32[256,768]{1,0:T(8,128)S(1)} %get-tuple-element.185, f32[768]{0:T(1024)S(1)} %reshape.432, f32[768]{0:T(1024)S(1)} %reshape.431, ...), kind=kOutput, calls=%fused_computation.13 | convolution fusion | flops 1260847104 | bytes 13389824 | tf_op jit(solution)/shard_map/dot_general | solution.py:861
  174.7 1.5 fusion.77
  179.0 1.1 fusion.66
  181.1 6.4 %convert_reduce_fusion = (f32[3072]{0:T(1024)}, bf16[256,3072]{1,0:T(8,128)(2,1)S(1)}) fusion(f32[256,3072]{1,0:T(8,128)S(1)} %copy-done.55, f32[256,3072]{1,0:T(8,128)} %get-tuple-element.186, bf16[256,768]{1,0:T(8,128)(2,1)S(1)} %get-tuple-element.46, bf16[3072,768]{1,0:T(8,128)(2,1)} %bitcast.257), kind=kOutput, calls=%fused_computation.11 | convolution fusion | flops 1220539392 | bytes 12988416 | tf_op jit(solution)/shard_map/dot_general | solution.py:37
  187.5 2.3 multiply_reduce_fusion
  190.9 1.9 convolution_convert_fusion.4
  193.6 12.0 %shard_map.284 = bf16[8,256,128]{2,1,0:T(8,128)(2,1)S(1)} custom-call(bf16[8,256,128]{2,1,0:T(8,128)(2,1)S(1)} %fusion.46.x_ref), custom_call_target="tpu_custom_call" | custom-call | tf_op jit(solution)/shard_map/pallas_call | solution.py:231
  206.6 1.7 copy.132
  209.5 1.2 copy.116.grad_ref
  210.7 20.4 %shard_map.285 = (f32[64,3072]{1,0:T(8,128)S(1)}, f32[2,2048,128]{2,1,0:T(8,128)}, f32[2,2048,64]{2,1,0:T(8,128)}) custom-call(bf16[3072,128]{1,0:T(8,128)(2,1)} %copy-done.5, bf16[2,2048,128]{2,1,0:T(8,128)(2,1)} %copy-done.3, bf16[2,64,2048]{2,1,0:T(8,128)(2,1)S(1)} %fusion.32.key_t_ref, bf16[2,2048,64]{2,1,0:T(8,128)(2,1)} %get-tuple-element.139.value_ref, ...), custom_call_target="tpu_custom_call" | custom-call | flops 4026531840 | bytes 12582912 | tf_op jit(solution)/shard_map/pallas_call | solution.py:523
  232.2 1.9 convert.15
  237.4 4.7 concatenate.153.x_ref
  242.1 31.4 %shard_map.286 = bf16[8,256,384]{2,1,0:T(8,128)(2,1)S(1)} custom-call(bf16[8,256,384]{2,1,0:T(8,128)(2,1)S(1)} %concatenate.153.x_ref), custom_call_target="tpu_custom_call" | custom-call | tf_op jit(solution)/shard_map/pallas_call | solution.py:231
  275.1 1.2 slice_bitcast_fusion.6
  277.3 3.1 concatenate.154
  280.5 4.3 fusion.17
  284.9 3.7 convolution_convert_fusion.2
  288.6 10.0 %reshape.412 = bf16[4,192,4,768]{3,2,1,0:T(4,128)(2,1)} reshape(bf16[768,3072]{1,0:T(8,128)(2,1)} %convolution_convert_fusion.2) | data formatting | bytes 9437184 | tf_op jit(solution)/shard_map/reshape | solution.py:431
  298.6 5.4 %copy.119 = bf16[4,192,4,768]{3,1,2,0:T(8,128)(2,1)} copy(bf16[4,192,4,768]{3,2,1,0:T(4,128)(2,1)} %reshape.412) | data formatting | bytes 9437184 | tf_op jit(solution)/shard_map/reshape | solution.py:431
  304.0 3.6 convolution_convert_fusion.1
  307.7 1.5 convolution_convert_fusion.3
  309.2 1.1 fusion
  310.3 4.0 copy.120
  314.3 8.8 %reshape.413 = bf16[4,192,3,768]{3,2,1,0:T(4,128)(2,1)} reshape(bf16[768,2304]{1,0:T(8,128)(2,1)} %copy.120) | data formatting | bytes 7077888 | tf_op jit(solution)/shard_map/reshape | solution.py:431
  323.1 3.0 copy.121
  326.1 2.5 pad_maximum_fusion
  328.6 121.7 %shard_map.287 = (bf16[2,4,96,768]{3,2,1,0:T(8,128)(2,1)S(1)}, bf16[2,4,96,768]{3,2,1,0:T(8,128)(2,1)S(1)}, bf16[2,4,96,768]{3,2,1,0:T(8,128)(2,1)S(1)}) custom-call(bf16[4,2,4,96,768]{4,3,2,1,0:T(8,128)(2,1)} %bitcast.262, bf16[4,2,4,96,768]{4,3,2,1,0:T(8,128)(2,1)} %bitcast.261, bf16[4,2,4,96,768]{4,3,2,1,0:T(8,128)(2,1)} %bitcast.263), custom_call_target="tpu_custom_call" | custom-call | tf_op jit(solution)/shard_map/pallas_call | solution.py:410
  450.3 1.9 bitcast_convert_fusion
  452.4 1.2 copy.122
  453.6 1.5 copy.134
  455.1 2.0 concatenate.156
  457.1 1.1 convert_reduce_fusion.5
  458.8 2.0 concatenate.157
  460.8 1.1 convert_reduce_fusion.4
  463.2 1.4 reshape.422
  466.0 1.3 reshape.425
  467.3 1.4 reshape.426
  469.3 1.4 concatenate.158
  470.8 41.5 %psum.7 = f32[4,2304]{1,0:T(4,128)} all-reduce(f32[4,2304]{1,0:T(4,128)} %concatenate.158), channel_id=1, replica_groups=mesh['fsdp'=4,'ctx'=8] {'fsdp','ctx'}, use_global_device_ids=true, to_apply=%region_18.19 | all-reduce | flops 9216 | bytes 73728 | tf_op jit(solution)/shard_map/psum | solution.py:909
  512.3 1.4 fusion.75
  514.8 1.7 copy.133
  516.5 1.4 dynamic-slice_reduce_fusion
  (224 shorter events, 34.5 us)
Async XLA Ops:
  19.8 26.0 %copy-start.33 = (bf16[256,768]{1,0:T(8,128)(2,1)S(1)}, bf16[256,768]{1,0:T(8,128)(2,1)}, u32[]{:S(2)}) copy-start(bf16[256,768]{1,0:T(8,128)(2,1)} %param.17) | copy-start | bytes 1179652
  43.5 2.1 copy-start
  53.4 4.4 copy-start.36
  53.4 4.4 copy-start.37
  58.0 1.3 copy-start.2
  89.6 2.2 copy-start.6
  96.4 1.4 copy-start.54
  97.7 8.4 %copy-start.5 = (bf16[3072,128]{1,0:T(8,128)(2,1)}, bf16[3072,128]{1,0:T(8,128)(2,1)S(1)}, u32[]{:S(2)}) copy-start(bf16[3072,128]{1,0:T(8,128)(2,1)S(1)} %maximum_maximum_fusion.query_ref) | copy-start | bytes 2359300
  98.8 0.8 copy-start.11
  98.8 1.0 copy-start.13
  102.4 3.7 copy-start.3
  119.1 38.6 %copy-start.4 = (f32[64,3072]{1,0:T(8,128)}, f32[64,3072]{1,0:T(8,128)S(1)}, u32[]{:S(2)}) copy-start(f32[64,3072]{1,0:T(8,128)S(1)} %get-tuple-element.28.out_ref) | copy-start | bytes 2359300
  119.1 2.9 copy-start.1
  119.5 0.8 copy-start.18
  120.6 39.9 %copy-start.34 = (bf16[256,768]{1,0:T(8,128)(2,1)S(1)}, bf16[256,768]{1,0:T(8,128)(2,1)}, u32[]{:S(2)}) copy-start(bf16[256,768]{1,0:T(8,128)(2,1)} %param.17) | copy-start | bytes 1179652
  157.7 2.2 copy-start.7
  159.9 3.1 copy-start.48
  160.5 14.1 %copy-start.21 = (bf16[256,768]{1,0:T(8,128)(2,1)}, bf16[256,768]{1,0:T(8,128)(2,1)S(1)}, u32[]{:S(2)}) copy-start(bf16[256,768]{1,0:T(8,128)(2,1)S(1)} %concatenate.137) | copy-start | bytes 1179652
  160.5 14.2 %slice-start.2 = ((s8[4718592]{0:T(1024)(128)(4,1)}), s8[524288]{0:T(1024)(128)(4,1)S(1)}, s32[]{:S(2)}) async-start(s8[4718592]{0:T(1024)(128)(4,1)} %bitcast.258), calls=%async_computation.2 | async-start | bytes 1048576
  162.6 12.0 %copy-start.38 = (f32[768]{0:T(1024)}, f32[768]{0:T(1024)S(1)}, u32[]{:S(2)}) copy-start(f32[768]{0:T(1024)S(1)} %reshape.432) | copy-start | bytes 9220
  162.7 12.0 %copy-start.40 = (f32[256]{0:T(256)}, f32[256]{0:T(256)S(1)}, u32[]{:S(2)}) copy-start(f32[256]{0:T(256)S(1)} %broadcast_multiply_fusion.2) | copy-start | bytes 3076
  162.9 11.7 %copy-start.49 = (f32[256]{0:T(256)}, f32[256]{0:T(256)S(1)}, u32[]{:S(2)}) copy-start(f32[256]{0:T(256)S(1)} %multiply_reduce_fusion.3) | copy-start | bytes 3076
  163.0 11.7 %copy-start.45 = (f32[256]{0:T(256)}, f32[256]{0:T(256)S(1)}, u32[]{:S(2)}) copy-start(f32[256]{0:T(256)S(1)} %fusion.59) | copy-start | bytes 3076
  163.0 11.7 %slice-start.3 = ((s8[4718592]{0:T(1024)(128)(4,1)}), s8[4194304]{0:T(1024)(128)(4,1)S(1)}, s32[]{:S(2)}) async-start(s8[4718592]{0:T(1024)(128)(4,1)} %bitcast.258), calls=%async_computation.3 | async-start | bytes 8388608
  163.0 11.7 %copy-start.51 = (f32[768]{0:T(1024)S(1)}, f32[768]{0:T(1024)}, u32[]{:S(2)}) copy-start(f32[768]{0:T(1024)} %reshape.434) | copy-start | bytes 9220
  174.7 1.6 copy-start.15
  174.7 2.6 copy-start.20
  176.3 3.9 copy-start.12
  176.3 3.9 copy-start.14
  179.0 2.0 copy-start.55
  180.1 7.3 %slice-start = ((s8[4718592]{0:T(1024)(128)(4,1)}), s8[4194304]{0:T(1024)(128)(4,1)S(1)}, s32[]{:S(2)}) async-start(s8[4718592]{0:T(1024)(128)(4,1)} %bitcast.254), calls=%async_computation | async-start | bytes 8388608
  181.0 6.4 %slice-start.1 = ((s8[4718592]{0:T(1024)(128)(4,1)}), s8[524288]{0:T(1024)(128)(4,1)S(1)}, s32[]{:S(2)}) async-start(s8[4718592]{0:T(1024)(128)(4,1)} %bitcast.254), calls=%async_computation.1 | async-start | bytes 1048576
  181.1 6.4 %copy-start.41 = (f32[256]{0:T(256)S(1)}, f32[256]{0:T(256)}, u32[]{:S(2)}) copy-start(f32[256]{0:T(256)} %copy-done.40) | copy-start | bytes 3076
  181.1 6.4 %copy-start.46 = (f32[256]{0:T(256)S(1)}, f32[256]{0:T(256)}, u32[]{:S(2)}) copy-start(f32[256]{0:T(256)} %copy-done.45) | copy-start | bytes 3076
  187.5 2.3 copy-start.25
  187.5 2.3 copy-start.50
  190.1 15.5 %copy-start.53 = (f32[256]{0:T(256)}, f32[256]{0:T(256)S(1)}, u32[]{:S(2)}) copy-start(f32[256]{0:T(256)S(1)} %negate_multiply_fusion.1) | copy-start | bytes 3076
  190.9 14.8 %copy-start.23 = (bf16[256,768]{1,0:T(8,128)(2,1)}, bf16[256,768]{1,0:T(8,128)(2,1)S(1)}, u32[]{:S(2)}) copy-start(bf16[256,768]{1,0:T(8,128)(2,1)S(1)} %get-tuple-element.50) | copy-start | bytes 1179652
  232.2 2.9 copy-start.19
  236.6 0.8 copy-start.17
  274.3 6.1 %copy-start.32 = (bf16[256,64]{1,0:T(8,128)(2,1)}, bf16[256,64]{1,0:T(8,128)(2,1)S(1)}, u32[]{:S(2)}) copy-start(bf16[256,64]{1,0:T(8,128)(2,1)S(1)} %get-tuple-element.85) | copy-start | bytes 98308
  277.3 7.5 %copy-start.27 = (bf16[256,64]{1,0:T(8,128)(2,1)}, bf16[256,64]{1,0:T(8,128)(2,1)S(1)}, u32[]{:S(2)}) copy-start(bf16[256,64]{1,0:T(8,128)(2,1)S(1)} %get-tuple-element.57) | copy-start | bytes 98308
  277.3 7.5 %copy-start.28 = (bf16[256,64]{1,0:T(8,128)(2,1)}, bf16[256,64]{1,0:T(8,128)(2,1)S(1)}, u32[]{:S(2)}) copy-start(bf16[256,64]{1,0:T(8,128)(2,1)S(1)} %get-tuple-element.58) | copy-start | bytes 98308
  277.3 7.5 %copy-start.29 = (bf16[256,64]{1,0:T(8,128)(2,1)}, bf16[256,64]{1,0:T(8,128)(2,1)S(1)}, u32[]{:S(2)}) copy-start(bf16[256,64]{1,0:T(8,128)(2,1)S(1)} %get-tuple-element.60) | copy-start | bytes 98308
  277.3 7.5 %copy-start.30 = (bf16[256,64]{1,0:T(8,128)(2,1)}, bf16[256,64]{1,0:T(8,128)(2,1)S(1)}, u32[]{:S(2)}) copy-start(bf16[256,64]{1,0:T(8,128)(2,1)S(1)} %get-tuple-element.65) | copy-start | bytes 98308
  277.3 7.6 %copy-start.31 = (bf16[256,64]{1,0:T(8,128)(2,1)}, bf16[256,64]{1,0:T(8,128)(2,1)S(1)}, u32[]{:S(2)}) copy-start(bf16[256,64]{1,0:T(8,128)(2,1)S(1)} %get-tuple-element.64) | copy-start | bytes 98308
  280.4 4.4 copy-start.8
  280.4 4.4 copy-start.26
  280.4 4.4 copy-start.39
  280.5 4.4 copy-start.42
  280.5 4.4 copy-start.47
  298.6 5.4 %copy-start.16 = (bf16[256,3072]{1,0:T(8,128)(2,1)S(1)}, bf16[256,3072]{1,0:T(8,128)(2,1)}, u32[]{:S(2)}) copy-start(bf16[256,3072]{1,0:T(8,128)(2,1)} %copy-done.15) | copy-start | bytes 4718596
  304.0 3.7 copy-start.22
  304.0 3.7 copy-start.24
  304.0 5.2 %copy-start.35 = (bf16[256,768]{1,0:T(8,128)(2,1)S(1)}, bf16[256,768]{1,0:T(8,128)(2,1)}, u32[]{:S(2)}) copy-start(bf16[256,768]{1,0:T(8,128)(2,1)} %param.17) | copy-start | bytes 1179652
  307.7 1.5 copy-start.9
  323.1 3.0 copy-start.10
  453.6 9.0 %copy-start.44 = (f32[768]{0:T(1024)S(1)}, f32[768]{0:T(1024)}, u32[]{:S(2)}) copy-start(f32[768]{0:T(1024)} %get-tuple-element.49) | copy-start | bytes 9220
  453.6 11.0 %copy-start.52 = (f32[768]{0:T(1024)S(1)}, f32[768]{0:T(1024)}, u32[]{:S(2)}) copy-start(f32[768]{0:T(1024)} %get-tuple-element.43) | copy-start | bytes 9220
  453.6 15.0 %copy-start.43 = (f32[768]{0:T(1024)S(1)}, f32[768]{0:T(1024)}, u32[]{:S(2)}) copy-start(f32[768]{0:T(1024)} %get-tuple-element.44) | copy-start | bytes 9220

commit v3 on v2

--- a/solution.py
+++ b/solution.py
@@ -428,13 +428,65 @@
 def split_wide(grad):
     rows, columns = grad.shape
     feat_width = HEADS * HEAD_DIM
-    parts = grad.reshape(4, rows // 4, columns // feat_width, feat_width)
-    return jnp.swapaxes(parts, 1, 2).reshape(4, -1, feat_width)
+    shards = grad.reshape(4, rows // 4, columns)
+    return jnp.concatenate(
+        [shards[:, :, at : at + feat_width] for at in range(0, columns, feat_width)], axis=1
+    )
 
 
 def join_wide(shard, rows):
-    parts = shard.reshape(-1, rows, shard.shape[1])
-    return jnp.swapaxes(parts, 0, 1).reshape(rows, -1)
+    return jnp.concatenate(
+        [shard[at : at + rows] for at in range(0, shard.shape[0], rows)], axis=1
+    )
+
+
+def bundle_kernel(n, x_ref, o_ref, near, far, send_sem, recv_sem):
+    f, c = lax.axis_index("fsdp"), lax.axis_index("ctx")
+    near_to = [lax.rem(f + step, 4) for step in range(1, 4)]
+    far_to = [{"ctx": lax.rem(c + step, n)} for step in range(1, n)]
+    greet([{"fsdp": peer} for peer in near_to] + far_to)
+    first = [
+        remote(x_ref.at[near_to[i]], near.at[i], send_sem.at[i], recv_sem.at[i], {"fsdp": near_to[i]})
+        for i in range(3)
+    ]
+    for one in first:
+        one.start()
+    for one in first:
+        one.wait()
+    far[c] = x_ref[f] + near[0] + near[1] + near[2]
+    for i in range(n - 1):
+        remote(
+            far.at[c], far.at[c], send_sem.at[3 + i], recv_sem.at[3 + i], far_to[i]
+        ).start()
+    for i in range(n - 1):
+        source = lax.rem(c + n - 1 - i, n)
+        remote(
+            far.at[source], far.at[source], send_sem.at[3 + i], recv_sem.at[3 + i], far_to[i]
+        ).wait()
+    total = far[0]
+    for i in range(1, n):
+        total = total + far[i]
+    o_ref[...] = total
+
+
+def reduce_bundle(bundle, n):
+    width = bundle.shape[1]
+    rows = -(-width // 1024) * 8
+    padded = jnp.pad(bundle, ((0, 0), (0, rows * 128 - width))).reshape(4, rows, 128)
+    total = pl.pallas_call(
+        functools.partial(bundle_kernel, n),
+        out_shape=jax.ShapeDtypeStruct((rows, 128), jnp.float32),
+        in_specs=vmem_specs(1),
+        out_specs=vmem_specs(1)[0],
+        scratch_shapes=[
+            pltpu.VMEM((3, rows, 128), jnp.float32),
+            pltpu.VMEM((n, rows, 128), jnp.float32),
+            pltpu.SemaphoreType.DMA((n + 2,)),
+            pltpu.SemaphoreType.DMA((n + 2,)),
+        ],
+        compiler_params=linked(7, 8),
+    )(padded)
+    return total.reshape(-1)[:width]
 
 
 QTILE = 512
@@ -906,8 +958,11 @@
         shift2_grad,
     )
     bundle = jnp.concatenate([total.reshape(n_fsdp, -1) for total in sums], axis=1)
-    bundle = lax.psum(bundle, ("fsdp", "ctx"))
-    bundle = lax.dynamic_index_in_dim(bundle, lax.axis_index("fsdp"), axis=0, keepdims=False)
+    if dealt:
+        bundle = reduce_bundle(bundle, n_ctx)
+    else:
+        bundle = lax.psum(bundle, ("fsdp", "ctx"))
+        bundle = lax.dynamic_index_in_dim(bundle, lax.axis_index("fsdp"), axis=0, keepdims=False)
     vector_parts = [bundle[ends[k] : ends[k + 1]] for k in range(len(sums))]
     if dealt:
         low = jnp.bfloat16

time: 527 us -> 452 us (0.86)
  local copies, waits for them, and re-layouts: 109 us -> 65.1 us
  blocking collectives: 51.2 us -> 9.65 us
  Pallas kernels: 288 us -> 299 us
    psum x1 -> x0, blocking collectives: 41.5 us -> none  [local(): bundle = lax.psum(bundle, ('fsdp', 'ctx'))]
    reshape x5 -> x0, local copies, waits for them, and re-layouts: 27 us -> none  [the longest x3 24.2 us: split_wide(): parts = grad.reshape(4, rows // 4, columns // feat_width, feat_width)]
    pallas_call x0 -> x1, Pallas kernels: none -> 10.8 us  [reduce_bundle(): pl.pallas_call(functools.partial(bundle_kernel, n), out_shape=jax.ShapeDt...]
    concatenate x0 -> x3, other arithmetic: none -> 5.62 us  [the longest x2 3.02 us: join_wide(): jnp.concatenate([shard[at:at + rows] for at in range(0, shard.shape[0], r...]
    reshape x9, local copies, waits for them, and re-layouts: 8.11 us -> 2.7 us  [local(): total.reshape(n_fsdp, -1)]
    unnamed x138 -> x159, local copies, waits for them, and re-layouts: 15.4 us -> 14 us
where the time goes in v3:
time: 452 us; the launch traced here: 444 us
  Pallas kernels  299 us (66%)
  local copies, waits for them, and re-layouts  65.1 us (14%)
  matrix products  39.6 us (9%)
  other arithmetic  27.1 us (6%)
  blocking collectives  9.65 us (2%)
    pallas_call x1, Pallas kernels, reduce_grads(): pl.pallas_call(reduce_kernel, out_shape=[jax.ShapeDtypeStruct((2, 4, piec...  122 us
    pallas_call x2, Pallas kernels, exchange_gather(): pl.pallas_call(functools.partial(swap_gather_kernel, n), out_shape=[jax.S...  65.9 us
    pallas_call x2, Pallas kernels, exchange(): pl.pallas_call(functools.partial(swap_kernel, n), out_shape=jax.ShapeDtyp...  43.4 us
    pallas_call x1, Pallas kernels, gather_kernel_call(): pl.pallas_call(gather_kernel, out_shape=jax.ShapeDtypeStruct((4, 2, rows...  23.6 us
    pallas_call x1, Pallas kernels, attend_back(): pl.pallas_call(functools.partial(attend_back_kernel, tiles_first), grid=(...  20.4 us
    dot_general x4, matrix products, back_dot(): lax.dot_general(first_op, second_op, (((1,), (1,)), ((), ())), preferred_...  14.6 us
    unnamed x159, local copies, waits for them, and re-layouts  14 us
    pallas_call x1, Pallas kernels, attend(): pl.pallas_call(attend_kernel, grid=(rows // QTILE,), in_specs=[pl.BlockSp...  12.9 us

profile of v3, /device:TPU:0, one launch (start us, length us, event | category | flops | bytes accessed | tf_op | source)
XLA Modules:
  0.0 443.6 jit_solution(2201845382310316847)
XLA Ops:
  0.6 6.1 %concatenate.129 = bf16[2304]{0:T(1024)(128)(2,1)S(1)} concatenate(bf16[192]{0:T(256)(128)(2,1)} %param.22, bf16[192]{0:T(256)(128)(2,1)} %param.23, bf16[192]{0:T(256)(128)(2,1)} %param.25, bf16[192]{0:T(256)(128)(2,1)} %param.26, bf16[192]{0:T(256)(128)(2,1)} %param.27, bf16[768]{0:T(1024)(128)(2,1)} %param.29, bf16[192]{0:T(256)(128)(2,1)} %param.31, bf16[192]{0:T(256)(128)(2,1)} %param.32, ...), dimensions={0} | concatenate | bytes 9216 | tf_op jit(solution)/shard_map/concatenate | solution.py:870
  6.8 9.6 %all-gather.1 = bf16[4,1,2304]{2,1,0:T(2,128)(2,1)S(1)} all-gather(bf16[1,1,2304]{2,1,0:T(2,128)(2,1)S(1)} %reshape.420), channel_id=2, replica_groups=mesh['fsdp'=4,'ctx'=8] {'fsdp'}, dimensions={0}, use_global_device_ids=true | all-gather | bytes 23040 | tf_op jit(solution)/shard_map/all_gather | solution.py:870
  18.5 1.4 pad_maximum_fusion.5
  19.9 23.6 %shard_map.280 = bf16[4,2,96,3072]{3,2,1,0:T(8,128)(2,1)S(1)} custom-call(bf16[2,96,3072]{2,1,0:T(8,128)(2,1)S(1)} %bitcast.239), custom_call_target="tpu_custom_call" | custom-call | tf_op jit(solution)/shard_map/pallas_call | solution.py:243
  43.5 2.2 copy-done
  45.9 3.1 fusion.1
  49.0 1.0 fusion.73
  50.2 1.1 concatenate.134
  51.3 1.0 concatenate.135
  52.4 1.1 fusion.72
  53.5 1.0 concatenate.136
  54.5 1.1 concatenate.137
  55.7 1.1 concatenate.138
  56.8 1.1 concatenate.139
  58.1 1.3 copy-done.2
  59.4 30.3 %shard_map.281 = (bf16[8,256,384]{2,1,0:T(8,128)(2,1)S(1)}, bf16[4,2,96,3072]{3,2,1,0:T(8,128)(2,1)S(1)}) custom-call(bf16[8,256,384]{2,1,0:T(8,128)(2,1)S(1)} %bitcast_dynamic-update-slice_fusion.x_ref, bf16[2,96,3072]{2,1,0:T(8,128)(2,1)S(1)} %bitcast.241), custom_call_target="tpu_custom_call" | custom-call | tf_op jit(solution)/shard_map/pallas_call | solution.py:257
  89.7 2.2 copy-done.6
  91.9 2.0 copy.72
  93.9 2.6 reshape.387
  99.8 1.1 pad_maximum_fusion.4
  100.9 1.6 copy.77.key_ref
  103.1 1.6 pad_maximum_fusion.6
  104.6 1.5 copy.78.value_ref
  106.2 12.9 %shard_map.282 = (f32[64,3072]{1,0:T(8,128)S(1)}, f32[1,3072]{1,0:T(1,128)S(1)}) custom-call(bf16[3072,128]{1,0:T(8,128)(2,1)S(1)} %maximum_maximum_fusion.query_ref, bf16[2,2048,128]{2,1,0:T(8,128)(2,1)S(1)} %copy.77.key_ref, bf16[2,64,2048]{2,1,0:T(8,128)(2,1)S(1)} %copy.78.value_ref), custom_call_target="tpu_custom_call" | custom-call | flops 1610612736 | bytes 8388608 | tf_op jit(solution)/shard_map/pallas_call | solution.py:510
  120.6 1.4 pad_maximum_fusion.9.x_ref
  122.0 35.7 %shard_map.283 = (bf16[8,256,128]{2,1,0:T(8,128)(2,1)S(1)}, bf16[4,2,384,768]{3,2,1,0:T(8,128)(2,1)S(1)}) custom-call(bf16[8,256,128]{2,1,0:T(8,128)(2,1)S(1)} %pad_maximum_fusion.9.x_ref, bf16[2,384,768]{2,1,0:T(8,128)(2,1)S(1)} %bitcast.240), custom_call_target="tpu_custom_call" | custom-call | tf_op jit(solution)/shard_map/pallas_call | solution.py:257
  157.7 2.2 copy-done.7
  160.6 2.0 fusion.79
  163.0 11.6 %multiply_convert_fusion = (bf16[256,3072]{1,0:T(8,128)(2,1)S(1)}, f32[256,3072]{1,0:T(8,128)}, f32[256,3072]{1,0:T(8,128)}) fusion(f32[3072]{0:T(1024)S(1)} %copy-done.59, bf16[768,3072]{1,0:T(8,128)(2,1)} %bitcast.243, f32[256,768]{1,0:T(8,128)S(1)} %get-tuple-element.200, f32[768]{0:T(1024)S(1)} %reshape.411, f32[768]{0:T(1024)S(1)} %reshape.410, ...), kind=kOutput, calls=%fused_computation.13 | convolution fusion | flops 1260847104 | bytes 13389824 | tf_op jit(solution)/shard_map/dot_general | solution.py:913
  174.8 1.5 fusion.80
  177.4 0.9 fusion.24
  179.1 1.1 fusion.65
  181.1 6.4 %convert_reduce_fusion = (f32[3072]{0:T(1024)}, bf16[256,3072]{1,0:T(8,128)(2,1)S(1)}) fusion(f32[256,3072]{1,0:T(8,128)S(1)} %copy-done.65, f32[256,3072]{1,0:T(8,128)} %get-tuple-element.201, bf16[256,768]{1,0:T(8,128)(2,1)S(1)} %get-tuple-element.46, bf16[3072,768]{1,0:T(8,128)(2,1)} %bitcast.247), kind=kOutput, calls=%fused_computation.11 | convolution fusion | flops 1220539392 | bytes 12988416 | tf_op jit(solution)/shard_map/dot_general | solution.py:37
  187.6 2.3 multiply_reduce_fusion
  190.9 1.9 convolution_convert_fusion.4
  193.7 12.0 %shard_map.284 = bf16[8,256,128]{2,1,0:T(8,128)(2,1)S(1)} custom-call(bf16[8,256,128]{2,1,0:T(8,128)(2,1)S(1)} %fusion.45.x_ref), custom_call_target="tpu_custom_call" | custom-call | tf_op jit(solution)/shard_map/pallas_call | solution.py:231
  206.6 1.7 copy.94
  208.6 1.0 fusion.60
  209.6 1.2 copy.83.grad_ref
  210.7 20.4 %shard_map.285 = (f32[64,3072]{1,0:T(8,128)S(1)}, f32[2,2048,128]{2,1,0:T(8,128)}, f32[2,2048,64]{2,1,0:T(8,128)}) custom-call(bf16[3072,128]{1,0:T(8,128)(2,1)} %copy-done.5, bf16[2,2048,128]{2,1,0:T(8,128)(2,1)} %copy-done.3, bf16[2,64,2048]{2,1,0:T(8,128)(2,1)S(1)} %fusion.31.key_t_ref, bf16[2,2048,64]{2,1,0:T(8,128)(2,1)} %get-tuple-element.154.value_ref, ...), custom_call_target="tpu_custom_call" | custom-call | flops 4026531840 | bytes 12582912 | tf_op jit(solution)/shard_map/pallas_call | solution.py:575
  231.2 1.0 copy.84
  232.2 1.9 convert.13
  234.1 1.0 fusion.75
  235.3 1.1 fusion.74
  237.5 4.7 %concatenate.162.x_ref = bf16[8,256,384]{2,1,0:T(8,128)(2,1)S(1)} concatenate(bf16[8,256,64]{2,1,0:T(8,128)(2,1)} %bitcast.257, bf16[8,256,64]{2,1,0:T(8,128)(2,1)} %bitcast.263, bf16[8,256,64]{2,1,0:T(8,128)(2,1)} %bitcast.265, bf16[8,256,64]{2,1,0:T(8,128)(2,1)} %bitcast.258, bf16[8,256,64]{2,1,0:T(8,128)(2,1)} %bitcast.262, bf16[8,256,64]{2,1,0:T(8,128)(2,1)} %bitcast.264), dimensions={2} | concatenate | bytes 3145728 | tf_op jit(solution)/shard_map/concatenate | solution.py:692
  242.2 31.4 %shard_map.286 = bf16[8,256,384]{2,1,0:T(8,128)(2,1)S(1)} custom-call(bf16[8,256,384]{2,1,0:T(8,128)(2,1)S(1)} %concatenate.162.x_ref), custom_call_target="tpu_custom_call" | custom-call | tf_op jit(solution)/shard_map/pallas_call | solution.py:231
  274.3 0.9 fusion.35
  275.2 1.2 slice_bitcast_fusion.6
  276.3 1.0 fusion.44
  277.3 3.1 concatenate.163
  280.5 4.0 fusion.16
  284.5 1.6 convolution_convert_fusion.2
  286.6 2.6 pad_maximum_fusion
  289.3 3.6 convolution_convert_fusion.1
  293.4 1.1 convolution_convert_fusion
  294.9 2.4 pad_maximum_fusion.1
  297.3 121.8 %shard_map.287 = (bf16[2,4,96,768]{3,2,1,0:T(8,128)(2,1)S(1)}, bf16[2,4,96,768]{3,2,1,0:T(8,128)(2,1)S(1)}, bf16[2,4,96,768]{3,2,1,0:T(8,128)(2,1)S(1)}) custom-call(bf16[4,2,4,96,768]{4,3,2,1,0:T(8,128)(2,1)} %bitcast.254, bf16[4,2,4,96,768]{4,3,2,1,0:T(8,128)(2,1)} %bitcast.251, bf16[4,2,4,96,768]{4,3,2,1,0:T(8,128)(2,1)} %bitcast.255), custom_call_target="tpu_custom_call" | custom-call | tf_op jit(solution)/shard_map/pallas_call | solution.py:410
  419.5 1.0 fusion.70
  420.5 1.3 pad_maximum_fusion.3
  421.8 1.2 concatenate.167
  423.2 1.2 concatenate.168
  427.3 10.8 %shard_map.288 = f32[24,128]{1,0:T(8,128)S(1)} custom-call(f32[4,24,128]{2,1,0:T(8,128)S(1)} %bitcast.242), custom_call_target="tpu_custom_call" | custom-call | tf_op jit(solution)/shard_map/pallas_call | solution.py:476
  438.8 1.9 bitcast_convert_fusion
  440.8 1.7 pad_maximum_fusion.2
  (244 shorter events, 22.4 us)
Async XLA Ops:
  19.8 26.0 %copy-start.42 = (bf16[256,768]{1,0:T(8,128)(2,1)S(1)}, bf16[256,768]{1,0:T(8,128)(2,1)}, u32[]{:S(2)}) copy-start(bf16[256,768]{1,0:T(8,128)(2,1)} %param.17) | copy-start | bytes 1179652
  43.5 2.2 copy-start
  53.5 4.4 copy-start.45
  53.5 4.4 copy-start.46
  89.7 2.2 copy-start.6
  97.8 8.4 %copy-start.5 = (bf16[3072,128]{1,0:T(8,128)(2,1)}, bf16[3072,128]{1,0:T(8,128)(2,1)S(1)}, u32[]{:S(2)}) copy-start(bf16[3072,128]{1,0:T(8,128)(2,1)S(1)} %maximum_maximum_fusion.query_ref) | copy-start | bytes 2359300
  102.5 3.7 copy-start.3
  119.1 38.6 %copy-start.4 = (f32[64,3072]{1,0:T(8,128)}, f32[64,3072]{1,0:T(8,128)S(1)}, u32[]{:S(2)}) copy-start(f32[64,3072]{1,0:T(8,128)S(1)} %get-tuple-element.28.out_ref) | copy-start | bytes 2359300
  119.1 2.9 copy-start.1
  120.6 39.9 %copy-start.43 = (bf16[256,768]{1,0:T(8,128)(2,1)S(1)}, bf16[256,768]{1,0:T(8,128)(2,1)}, u32[]{:S(2)}) copy-start(bf16[256,768]{1,0:T(8,128)(2,1)} %param.17) | copy-start | bytes 1179652
  157.7 2.2 copy-start.7
  159.9 3.1 copy-start.59
  160.6 14.1 %copy-start.18 = (bf16[256,768]{1,0:T(8,128)(2,1)}, bf16[256,768]{1,0:T(8,128)(2,1)S(1)}, u32[]{:S(2)}) copy-start(bf16[256,768]{1,0:T(8,128)(2,1)S(1)} %concatenate.146) | copy-start | bytes 1179652
  160.6 14.1 %slice-start.2 = ((s8[4718592]{0:T(1024)(128)(4,1)}), s8[524288]{0:T(1024)(128)(4,1)S(1)}, s32[]{:S(2)}) async-start(s8[4718592]{0:T(1024)(128)(4,1)} %bitcast.248), calls=%async_computation.2 | async-start | bytes 1048576
  162.7 12.0 %copy-start.47 = (f32[768]{0:T(1024)}, f32[768]{0:T(1024)S(1)}, u32[]{:S(2)}) copy-start(f32[768]{0:T(1024)S(1)} %reshape.411) | copy-start | bytes 9220
  162.8 11.9 %copy-start.49 = (f32[256]{0:T(256)}, f32[256]{0:T(256)S(1)}, u32[]{:S(2)}) copy-start(f32[256]{0:T(256)S(1)} %broadcast_multiply_fusion.2) | copy-start | bytes 3076
  163.0 11.7 %copy-start.60 = (f32[256]{0:T(256)}, f32[256]{0:T(256)S(1)}, u32[]{:S(2)}) copy-start(f32[256]{0:T(256)S(1)} %multiply_reduce_fusion.3) | copy-start | bytes 3076
  163.0 11.7 %copy-start.56 = (f32[256]{0:T(256)}, f32[256]{0:T(256)S(1)}, u32[]{:S(2)}) copy-start(f32[256]{0:T(256)S(1)} %fusion.58) | copy-start | bytes 3076
  163.0 11.7 %slice-start.3 = ((s8[4718592]{0:T(1024)(128)(4,1)}), s8[4194304]{0:T(1024)(128)(4,1)S(1)}, s32[]{:S(2)}) async-start(s8[4718592]{0:T(1024)(128)(4,1)} %bitcast.248), calls=%async_computation.3 | async-start | bytes 8388608
  163.0 11.7 %copy-start.62 = (f32[768]{0:T(1024)S(1)}, f32[768]{0:T(1024)}, u32[]{:S(2)}) copy-start(f32[768]{0:T(1024)} %reshape.413) | copy-start | bytes 9220
  174.7 1.6 copy-start.12
  174.8 2.6 copy-start.17
  176.3 3.9 copy-start.9
  176.3 3.9 copy-start.11
  179.1 2.0 copy-start.65
  180.2 7.3 %slice-start = ((s8[4718592]{0:T(1024)(128)(4,1)}), s8[4194304]{0:T(1024)(128)(4,1)S(1)}, s32[]{:S(2)}) async-start(s8[4718592]{0:T(1024)(128)(4,1)} %bitcast.244), calls=%async_computation | async-start | bytes 8388608
  181.1 6.4 %slice-start.1 = ((s8[4718592]{0:T(1024)(128)(4,1)}), s8[524288]{0:T(1024)(128)(4,1)S(1)}, s32[]{:S(2)}) async-start(s8[4718592]{0:T(1024)(128)(4,1)} %bitcast.244), calls=%async_computation.1 | async-start | bytes 1048576
  181.1 6.4 %copy-start.50 = (f32[256]{0:T(256)S(1)}, f32[256]{0:T(256)}, u32[]{:S(2)}) copy-start(f32[256]{0:T(256)} %copy-done.49) | copy-start | bytes 3076
  181.1 6.4 %copy-start.57 = (f32[256]{0:T(256)S(1)}, f32[256]{0:T(256)}, u32[]{:S(2)}) copy-start(f32[256]{0:T(256)} %copy-done.56) | copy-start | bytes 3076
  187.5 2.3 copy-start.22
  187.5 2.3 copy-start.61
  190.2 15.5 %copy-start.63 = (f32[256]{0:T(256)}, f32[256]{0:T(256)S(1)}, u32[]{:S(2)}) copy-start(f32[256]{0:T(256)S(1)} %negate_multiply_fusion.1) | copy-start | bytes 3076
  190.9 14.8 %copy-start.20 = (bf16[256,768]{1,0:T(8,128)(2,1)}, bf16[256,768]{1,0:T(8,128)(2,1)S(1)}, u32[]{:S(2)}) copy-start(bf16[256,768]{1,0:T(8,128)(2,1)S(1)} %get-tuple-element.50) | copy-start | bytes 1179652
  232.2 2.9 copy-start.16
  274.3 6.1 %copy-start.34 = (bf16[256,64]{1,0:T(8,128)(2,1)}, bf16[256,64]{1,0:T(8,128)(2,1)S(1)}, u32[]{:S(2)}) copy-start(bf16[256,64]{1,0:T(8,128)(2,1)S(1)} %get-tuple-element.100) | copy-start | bytes 98308
  277.3 7.2 %copy-start.24 = (bf16[256,64]{1,0:T(8,128)(2,1)}, bf16[256,64]{1,0:T(8,128)(2,1)S(1)}, u32[]{:S(2)}) copy-start(bf16[256,64]{1,0:T(8,128)(2,1)S(1)} %get-tuple-element.72) | copy-start | bytes 98308
  277.3 7.2 %copy-start.26 = (bf16[256,64]{1,0:T(8,128)(2,1)}, bf16[256,64]{1,0:T(8,128)(2,1)S(1)}, u32[]{:S(2)}) copy-start(bf16[256,64]{1,0:T(8,128)(2,1)S(1)} %get-tuple-element.73) | copy-start | bytes 98308
  277.3 7.2 %copy-start.28 = (bf16[256,64]{1,0:T(8,128)(2,1)}, bf16[256,64]{1,0:T(8,128)(2,1)S(1)}, u32[]{:S(2)}) copy-start(bf16[256,64]{1,0:T(8,128)(2,1)S(1)} %get-tuple-element.75) | copy-start | bytes 98308
  277.3 7.2 %copy-start.30 = (bf16[256,64]{1,0:T(8,128)(2,1)}, bf16[256,64]{1,0:T(8,128)(2,1)S(1)}, u32[]{:S(2)}) copy-start(bf16[256,64]{1,0:T(8,128)(2,1)S(1)} %get-tuple-element.80) | copy-start | bytes 98308
  277.3 7.2 %copy-start.32 = (bf16[256,64]{1,0:T(8,128)(2,1)}, bf16[256,64]{1,0:T(8,128)(2,1)S(1)}, u32[]{:S(2)}) copy-start(bf16[256,64]{1,0:T(8,128)(2,1)S(1)} %get-tuple-element.79) | copy-start | bytes 98308
  280.4 4.1 copy-start.23
  280.5 4.1 copy-start.48
  280.5 4.1 copy-start.51
  280.5 4.1 copy-start.58
  286.6 2.6 copy-start.13
  289.3 3.7 copy-start.19
  289.3 3.7 copy-start.21
  289.3 4.2 copy-start.44
  419.4 2.4 copy-start.33
  419.4 2.4 copy-start.36
  419.4 2.4 copy-start.37
  419.4 2.4 copy-start.38
  419.4 2.4 copy-start.39
  419.4 2.4 copy-start.40
  419.4 2.4 copy-start.41
  420.4 2.8 copy-start.25
  420.4 2.8 copy-start.27
  420.4 2.8 copy-start.29
  420.4 2.8 copy-start.31
  420.4 2.8 copy-start.35
  420.4 4.1 copy-start.55
  420.5 6.4 %copy-start.54 = (f32[768]{0:T(1024)S(1)}, f32[768]{0:T(1024)}, u32[]{:S(2)}) copy-start(f32[768]{0:T(1024)} %get-tuple-element.45) | copy-start | bytes 9220
  420.5 6.5 %copy-start.53 = (f32[768]{0:T(1024)S(1)}, f32[768]{0:T(1024)}, u32[]{:S(2)}) copy-start(f32[768]{0:T(1024)} %get-tuple-element.41) | copy-start | bytes 9220
  420.5 6.6 %copy-start.52 = (f32[768]{0:T(1024)S(1)}, f32[768]{0:T(1024)}, u32[]{:S(2)}) copy-start(f32[768]{0:T(1024)} %get-tuple-element.44) | copy-start | bytes 9220
  (6 other events, 6.0 us)
